TPU v7x, 32 devices: a whole 2x2x4 slice. The times are simulated.
32 devices in a mesh: ctx: 8 (over y, x, core), head: 4 (over z).
Axes of the slice: x: 2, y: 2, z: 4, core: 2. Of those that a mesh axis runs over, the one named last changes fastest.
Arguments:
- queries: bfloat16 [4096, 4096], P('ctx', 'head'), may hold values from -0.59765625 to 0.59765625
- keys: bfloat16 [4096, 4096], P('ctx', 'head'), may hold values from -0.59765625 to 0.59765625
- values: bfloat16 [4096, 4096], P('ctx', 'head'), may hold values from -6 to 6
- gates: float32 [32, 7, 4096], P('head', None, 'ctx'), may hold values from 0.05 to 1
- segment_ids: int32 [4096], P('ctx'), may hold values from 0 to 2, never falling along the last dimension, each value on 1 to 3072 neighbouring positions
- out_weight: bfloat16 [4096, 4096], P('head'), may hold values from -0.09375 to 0.09375
- out_grad: bfloat16 [4096, 4096], P('ctx', 'head'), may hold values from -0.59765625 to 0.59765625
Outputs:
- mixed: bfloat16 [4096, 4096], P('ctx', 'head')
- grad_queries: bfloat16 [4096, 4096], P('ctx', 'head')
- grad_keys: bfloat16 [4096, 4096], P('ctx', 'head')
- grad_values: bfloat16 [4096, 4096], P('ctx', 'head')
Inputs may be any that keep to these rules, and one draw needn't show every extreme that they name: `segment_ids`: segment ids never fall along the sequence: each document is one run of consecutive tokens; one document has exactly 3072 tokens.
All inputs are finite; a program needn't handle non-finite values.
Results may differ from a plain program's by a relative error of at most 0.018.
Values may be sent and summed in bfloat16 or wider, within the bound.
A program may use at most 64 MiB of HBM per device.

v0:
```python
import jax
import jax.numpy as jnp
from jax import lax
from jax.sharding import PartitionSpec as P

SPAN = 64


def from_partner(value, axis, distance):
    mask = 2**distance
    pairs = [(source, source ^ mask) for source in range(lax.axis_size(axis))]
    return lax.ppermute(value, axis, pairs)


def level_table(count, near_count):
    span_ids = jnp.arange(count, dtype=jnp.int32) // SPAN
    differ = jnp.bitwise_xor(span_ids[:, None], span_ids[None, :])
    levels = jnp.zeros((count, count), jnp.int32)
    for section in range(near_count - 1):
        levels = levels + (differ >= 1 << section).astype(jnp.int32)
    return levels


def split_product(form, rows, state):
    upper = state.astype(jnp.bfloat16)
    lower = (state - upper.astype(jnp.float32)).astype(jnp.bfloat16)
    first = jnp.einsum(form, rows, upper, preferred_element_type=jnp.float32)
    return first + jnp.einsum(form, rows, lower, preferred_element_type=jnp.float32)


def pair_update(partner, partner_mark, block_state, block_mark, is_upper, first_value):
    linked = partner_mark[0] == first_value
    piece = jnp.where(is_upper & linked, partner, jnp.float32(0))
    joined = partner_mark[0] == block_mark[0]
    lower_state = jnp.where(is_upper, partner, block_state)
    upper_state = jnp.where(is_upper, block_state, partner)
    new_state = jnp.where(joined, lower_state, jnp.float32(0)) + upper_state
    new_mark = jnp.where(is_upper, block_mark, partner_mark)
    return (piece, new_state, new_mark)


def dual_update(partner, partner_mark, dual_state, dual_mark, inbound, is_upper, last_value):
    linked = partner_mark[0] == last_value
    inbound = inbound + jnp.where(jnp.logical_not(is_upper) & linked, partner[0], jnp.float32(0))
    joined = partner_mark[0] == dual_mark[0]
    lower_state = jnp.where(is_upper, partner, dual_state)
    upper_state = jnp.where(is_upper, dual_state, partner)
    new_state = lower_state[1:] + jnp.where(joined, upper_state[1:], jnp.float32(0))
    new_mark = jnp.where(is_upper, partner_mark, dual_mark)
    return (inbound, new_state, new_mark)


def shards(queries, keys, values, gates, segment_ids, out_weight, out_grad):
    row_count = queries.shape[0]
    heads_here = gates.shape[0]
    key_width = queries.shape[1] // heads_here
    value_width = values.shape[1] // heads_here
    near_count = (row_count // SPAN).bit_length()
    spread = lax.axis_size("ctx").bit_length() - 1
    my_index = lax.axis_index("ctx")
    query_heads = queries.reshape(row_count, heads_here, key_width)
    key_heads = keys.reshape(row_count, heads_here, key_width)
    value_heads = values.reshape(row_count, heads_here, value_width)
    levels = level_table(row_count, near_count)
    positions = jnp.arange(row_count, dtype=jnp.int32)
    allowed = (positions[:, None] >= positions[None, :]) & (
        segment_ids[:, None] == segment_ids[None, :]
    )
    weight = jnp.zeros((heads_here, row_count, row_count), jnp.float32)
    for level_id in range(near_count):
        weight = weight + jnp.where(levels == level_id, gates[:, level_id, :, None], jnp.float32(0))
    weight = jnp.where(allowed, weight, jnp.float32(0))
    scores = jnp.einsum("thd,shd->hts", query_heads, key_heads, preferred_element_type=jnp.float32)
    near_probs = (weight * scores).astype(jnp.bfloat16)
    near_out = jnp.einsum(
        "hts,she->the", near_probs, value_heads, preferred_element_type=jnp.float32
    )
    first_seg = segment_ids[0]
    last_seg = segment_ids[row_count - 1]
    first_mark = first_seg.astype(jnp.float32)[None]
    last_mark = last_seg.astype(jnp.float32)[None]
    low_keep = segment_ids == last_seg
    high_keep = (segment_ids == first_seg).astype(jnp.float32)
    masked_keys = jnp.where(low_keep[:, None, None], key_heads, jnp.zeros((), jnp.bfloat16))
    summary = jnp.einsum(
        "thd,the->hde", masked_keys, value_heads, preferred_element_type=jnp.float32
    )
    grad_attention = jnp.einsum(
        "tc,rc->tr",
        lax.all_gather(out_grad, "head", axis=1, tiled=True),
        out_weight,
        preferred_element_type=jnp.float32,
    ).astype(jnp.bfloat16)
    grad_heads = grad_attention.reshape(row_count, heads_here, value_width)
    value_scores = jnp.einsum(
        "the,she->hts", grad_heads, value_heads, preferred_element_type=jnp.float32
    )
    grad_scores = (weight * value_scores).astype(jnp.bfloat16)
    near_dq = jnp.einsum("hts,shd->thd", grad_scores, key_heads, preferred_element_type=jnp.float32)
    near_dk = jnp.einsum(
        "hts,thd->shd", grad_scores, query_heads, preferred_element_type=jnp.float32
    )
    near_dv = jnp.einsum("hts,the->she", near_probs, grad_heads, preferred_element_type=jnp.float32)
    far_gate = gates[:, near_count:, :] * high_keep[None, None, :]
    scaled_grad = (
        far_gate[:, :, :, None] * grad_heads.astype(jnp.float32).transpose(1, 0, 2)[:, None]
    )
    leaves = split_product("thd,hjte->jhde", query_heads, scaled_grad)
    first_value = first_mark[0]
    last_value = last_mark[0]
    inbound = jnp.zeros((heads_here, key_width, value_width), jnp.float32)
    block_state = summary
    block_mark = last_mark
    pieces = []
    for section in range(spread):
        partner, partner_mark = (
            from_partner(block_state.astype(jnp.bfloat16), "ctx", section).astype(
                block_state.dtype
            ),
            from_partner(block_mark.astype(jnp.bfloat16), "ctx", section).astype(block_mark.dtype),
        )
        is_upper = my_index >> section & 1 == 1
        piece, block_state, block_mark = pair_update(
            partner, partner_mark, block_state, block_mark, is_upper, first_value
        )
        pieces.append(piece)
    incoming = jnp.stack(pieces)
    dual_state = leaves
    dual_mark = first_mark
    for section in range(spread):
        partner, partner_mark = (
            from_partner(dual_state.astype(jnp.bfloat16), "ctx", section).astype(dual_state.dtype),
            from_partner(dual_mark.astype(jnp.bfloat16), "ctx", section).astype(dual_mark.dtype),
        )
        is_upper = my_index >> section & 1 == 1
        inbound, dual_state, dual_mark = dual_update(
            partner, partner_mark, dual_state, dual_mark, inbound, is_upper, last_value
        )
    projected = split_product("thd,jhde->hjte", query_heads, incoming)
    far_out = jnp.sum(far_gate[:, :, :, None] * projected, axis=1).transpose(1, 0, 2)
    attention = (
        (near_out + far_out).astype(jnp.bfloat16).reshape(row_count, heads_here * value_width)
    )
    partial_value = jnp.dot(attention, out_weight, preferred_element_type=jnp.float32)
    mixed = lax.psum_scatter(
        partial_value.astype(jnp.bfloat16), "head", scatter_dimension=1, tiled=True
    )
    carried = split_product("the,jhde->hjtd", grad_heads, incoming)
    far_dq = jnp.sum(far_gate[:, :, :, None] * carried, axis=1).transpose(1, 0, 2)
    low_mask = low_keep.astype(jnp.float32)[:, None, None]
    far_dk = split_product("the,hde->thd", value_heads, inbound) * low_mask
    far_dv = split_product("thd,hde->the", key_heads, inbound) * low_mask
    grad_queries = (
        (near_dq + far_dq).astype(jnp.bfloat16).reshape(row_count, heads_here * key_width)
    )
    grad_keys = (near_dk + far_dk).astype(jnp.bfloat16).reshape(row_count, heads_here * key_width)
    grad_values = (
        (near_dv + far_dv).astype(jnp.bfloat16).reshape(row_count, heads_here * value_width)
    )
    return (mixed, grad_queries, grad_keys, grad_values)


def solution(mesh):
    placed = (
        P("ctx", "head"),
        P("ctx", "head"),
        P("ctx", "head"),
        P("head", None, "ctx"),
        P("ctx"),
        P("head", None),
        P("ctx", "head"),
    )
    return jax.shard_map(
        shards,
        mesh=mesh,
        in_specs=placed,
        out_specs=(P("ctx", "head"), P("ctx", "head"), P("ctx", "head"), P("ctx", "head")),
        check_vma=False,
    )
```

profile of v0, /device:TPU:0, one launch (start us, length us, event | category | flops | bytes accessed | tf_op | source)
XLA Modules:
  0.0 178.1 jit_solution(14406610596685351762)
XLA Ops:
  8.0 1.5 copy.70
  10.9 1.3 fusion.72
  14.8 1.9 %fusion.31 = (pred[512,512]{1,0:T(8,128)(4,1)}, pred[512,512]{1,0:T(8,128)(4,1)}, pred[512,512]{1,0:T(8,128)(4,1)}, pred[512,512]{1,0:T(8,128)(4,1)}) fusion(s32[512]{0:T(512)S(1)} %add_select_fusion.1), kind=kLoop, calls=%fused_computation.50 | loop fusion | flops 3407872 | bytes 1050624 | tf_op jit(solution)/shard_map/eq | solution.py:71
  18.2 2.9 %collective-permute-start.3 = (bf16[8,128,128]{2,1,0:T(8,128)(2,1)}, bf16[8,128,128]{2,1,0:T(8,128)(2,1)}, u32[]{:S(2)}, u32[]{:S(2)}) collective-permute-start(bf16[8,128,128]{2,1,0:T(8,128)(2,1)} %fusion.65), channel_id=1, source_target_pairs={{0,8},{4,12},{8,0},{12,4},{16,24},{20,28},{24,16},{28,20},{1,9},{5... | collective-permute-start | bytes 786440 | tf_op jit(solution)/shard_map/ppermute | solution.py:12
  22.4 1.5 copy.69
  24.0 1.5 copy.28
  27.0 1.4 collective-permute-start.2
  28.4 2.2 %collective-permute-done.2 = bf16[1]{0:T(256)(128)(2,1)} collective-permute-done((bf16[1]{0:T(256)(128)(2,1)}, bf16[1]{0:T(256)(128)(2,1)}, u32[]{:S(2)}, u32[]{:S(2)}) %collective-permute-start.2) | collective-permute-done | bytes 34 | tf_op jit(solution)/shard_map/ppermute | solution.py:12
  31.2 2.1 %fusion.54 = (f32[1,8,128,128]{3,2,1,0:T(8,128)S(1)}, bf16[8,128,128]{2,1,0:T(8,128)(2,1)}, f32[1,8,128,128]{3,2,1,0:T(8,128)S(1)}) fusion(bf16[8,128,128]{2,1,0:T(8,128)(2,1)S(1)} %collective-permute-done.1, pred[]{:T(512)S(6)} %and.64, f32[8,128,128]{2,1,0:T(8,128)} %copy-done.17, pred[]{:T(512)} %eq.96, pred[]{:T(512)S(6)} %eq.102, ...), kind=kLoop, calls=%fused_computation.80 | loop fusion | flops 1703936 | bytes 2359302 | tf_op jit(solution)/shard_map/stack | solution.py:127
  33.3 1.6 collective-permute-start.5
  34.9 8.4 %multiply_convert_fusion.2 = bf16[8,512,512]{2,1,0:T(8,128)(2,1)} fusion(f32[8,512]{1,0:T(8,128)S(1)} %copy-done.28, f32[8,512]{1,0:T(8,128)S(1)} %copy-done.26, f32[8,512]{1,0:T(8,128)S(1)} %copy-done.27, f32[8,512]{1,0:T(8,128)S(1)} %get-tuple-element.15, pred[512,512]{1,0:T(8,128)(4,1)} %get-tuple-element.20, pred[512,512]{1,0:T(8,128)(4,1)} %get-tuple-element.22, ...), kind=kOutput, calls=%fused_computation.3 | convolution fusion | flops 557842432 | bytes 7667712 | tf_op jit(solution)/shard_map/thd,shd->hts/dot_general | solution.py:73
  44.7 1.8 %collective-permute-start.4 = (bf16[1]{0:T(256)(128)(2,1)}, bf16[1]{0:T(256)(128)(2,1)}, u32[]{:S(2)}, u32[]{:S(2)}) collective-permute-start(bf16[1]{0:T(256)(128)(2,1)} %select_n.196), channel_id=1, source_target_pairs={{0,16},{4,20},{8,24},{12,28},{16,0},{20,4},{24,8},{28,12},{1,17},{... | collective-permute-start | bytes 14 | tf_op jit(solution)/shard_map/ppermute | solution.py:12
  46.6 1.8 collective-permute-done.4
  49.0 1.0 fusion.43
  50.1 1.3 multiply_reduce_fusion.1
  51.5 1.3 copy-done.1
  52.7 1.5 fusion.10
  54.3 6.4 %convolution_convert_fusion = bf16[512,4096]{1,0:T(8,128)(2,1)} fusion(bf16[512,1024]{0,1:T(8,128)(2,1)S(1)} %bitcast.149, bf16[1024,4096]{1,0:T(8,128)(2,1)S(1)} %bitcast.151), kind=kOutput, calls=%fused_computation.8 | convolution fusion | flops 4297064448 | bytes 13631488 | tf_op jit(solution)/shard_map/dot_general | solution.py:144
  63.3 1.9 %collective-permute-start.8 = (bf16[1]{0:T(256)(128)(2,1)}, bf16[1]{0:T(256)(128)(2,1)}, u32[]{:S(2)}, u32[]{:S(2)}) collective-permute-start(bf16[1]{0:T(256)(128)(2,1)} %convert_element_type.209), channel_id=1, source_target_pairs={{0,8},{4,12},{8,0},{12,4},{16,24},{20,28},{24,16},{28,20},{1,9},{5... | collective-permute-start | bytes 14 | tf_op jit(solution)/shard_map/ppermute | solution.py:12
  65.2 1.8 collective-permute-done.8
  68.2 1.8 %collective-permute-start.10 = (bf16[1]{0:T(256)(128)(2,1)}, bf16[1]{0:T(256)(128)(2,1)}, u32[]{:S(2)}, u32[]{:S(2)}) collective-permute-start(bf16[1]{0:T(256)(128)(2,1)} %select_n.214), channel_id=1, source_target_pairs={{0,16},{4,20},{8,24},{12,28},{16,0},{20,4},{24,8},{28,12},{1,17},{... | collective-permute-start | bytes 14 | tf_op jit(solution)/shard_map/ppermute | solution.py:12
  70.1 1.9 %collective-permute-done.10 = bf16[1]{0:T(256)(128)(2,1)} collective-permute-done((bf16[1]{0:T(256)(128)(2,1)}, bf16[1]{0:T(256)(128)(2,1)}, u32[]{:S(2)}, u32[]{:S(2)}) %collective-permute-start.10) | collective-permute-done | bytes 34 | tf_op jit(solution)/shard_map/ppermute | solution.py:12
  72.6 20.5 %all-gather.2.cloned.1.call-done = bf16[512,4096]{1,0:T(8,128)(2,1)} async-done(((bf16[512,1024]{1,0:T(8,128)(2,1)}), bf16[512,4096]{1,0:T(8,128)(2,1)}) %all-gather.2.cloned.1.call-update) | async-done | bytes 4194320 | tf_op jit(solution)/shard_map/all_gather | solution.py:90
  93.1 9.2 %fusion.13 = bf16[64,8,8,128]{3,1,2,0:T(8,128)(2,1)S(1)} fusion(bf16[512,4096]{1,0:T(8,128)(2,1)} %all-gather.2.cloned.1.call-done, bf16[1024,4096]{1,0:T(8,128)(2,1)} %param.12), kind=kOutput, calls=%fused_computation.30 | convolution fusion | flops 4295491584 | bytes 13631488 | tf_op jit(solution)/shard_map/tc,rc->tr/dot_general | solution.py:88
  102.5 1.5 copy.37
  104.0 1.5 convert_bitcast_fusion
  105.6 2.9 %copy.30 = f32[8,512,128]{1,2,0:T(8,128)} copy(f32[8,512,128]{2,0,1:T(8,128)} %convert_bitcast_fusion) | data formatting | bytes 4194304 | tf_op jit(solution)/shard_map/transpose | solution.py:106
  108.5 2.8 %fusion.1 = f32[8,3,128,128]{3,2,1,0:T(8,128)S(1)} fusion(f32[8,512,128]{1,2,0:T(8,128)} %copy.30, f32[8,3,512]{2,1,0:T(4,128)S(1)} %copy.14, bf16[512,8,128,1]{2,1,0,3:T(8,128)(2,1)S(1)} %bitcast.141), kind=kOutput, calls=%fused_computation.9 | convolution fusion | flops 405798912 | bytes 4767744 | tf_op jit(solution)/shard_map/thd,hjte->jhde/dot_general | solution.py:27
  111.3 1.0 fusion.76
  114.2 5.8 %multiply_convert_fusion.1 = bf16[8,512,512]{2,1,0:T(8,128)(2,1)S(1)} fusion(f32[8,512]{1,0:T(8,128)S(1)} %copy-done.28, f32[8,512]{1,0:T(8,128)S(1)} %copy-done.26, f32[8,512]{1,0:T(8,128)S(1)} %copy-done.27, f32[8,512]{1,0:T(8,128)S(1)} %get-tuple-element.15, pred[512,512]{1,0:T(8,128)(4,1)S(1)} %copy-done.21, pred[512,512]{1,0:T(8,128)(4,1)S(1)} %copy-done.23, ...), kind=kOutput, calls=%fused_computation.2 | convolution fusion | flops 557842432 | bytes 7667712 | tf_op jit(solution)/shard_map/the,she->hts/dot_general | solution.py:95
  120.2 1.7 fusion.73
  122.0 1.5 collective-permute-start.9
  123.4 1.1 multiply_reduce_fusion
  124.6 1.5 fusion.9
  126.1 1.5 copy.40
  127.6 8.7 %collective-permute-done.9 = bf16[2,8,128,128]{2,3,0,1:T(8,128)(2,1)} collective-permute-done((bf16[2,8,128,128]{2,3,0,1:T(8,128)(2,1)}, bf16[2,8,128,128]{2,3,0,1:T(8,128)(2,1)}, u32[]{:S(2)}, u32[]{:S(2)}) %collective-permute-start.9) | collective-permute-done | bytes 524320 | tf_op jit(solution)/shard_map/ppermute | solution.py:12
  136.4 1.1 convert_element_type.212
  137.5 1.1 add_convert_fusion.1
  138.7 1.5 collective-permute-start.11
  140.2 4.3 %fusion.77 = f32[8,128,512]{2,1,0:T(8,128)} fusion(bf16[512,8,128]{0,2,1:T(8,128)(2,1)S(1)} %copy-done.13, bf16[8,512,512]{2,1,0:T(8,128)(2,1)} %multiply_convert_fusion.2), kind=kOutput, calls=%fused_computation.119 | convolution fusion | flops 536870912 | bytes 7340032 | tf_op jit(solution)/shard_map/hts,the->she/dot_general | solution.py:103
  144.5 1.9 %collective-permute-done.11 = bf16[1,8,128,128]{2,3,0,1:T(8,128)(2,1)S(1)} collective-permute-done((bf16[1,8,128,128]{2,3,0,1:T(8,128)(2,1)S(1)}, bf16[1,8,128,128]{2,3,0,1:T(8,128)(2,1)S(1)}, u32[]{:S(2)}, u32[]{:S(2)}) %collective-permute-start.11) | collective-permute-done | bytes 262176 | tf_op jit(solution)/shard_map/ppermute | solution.py:12
  146.4 1.2 fusion.63
  148.6 1.7 fusion.8
  150.3 2.3 %copy.41 = bf16[512,1024]{1,0:T(8,128)(2,1)} copy(bf16[512,1024]{0,1:T(8,128)(2,1)} %bitcast.146) | data formatting | bytes 2097152
  153.1 1.1 copy-done.11
  154.2 1.6 add_convert_fusion
  155.8 2.3 %copy.42 = bf16[512,1024]{1,0:T(8,128)(2,1)} copy(bf16[512,1024]{0,1:T(8,128)(2,1)} %bitcast.144) | data formatting | bytes 2097152
  158.0 13.2 %reduce-scatter.2.cloned.1.call-done = bf16[512,1024]{1,0:T(8,128)(2,1)} async-done(((bf16[512,4096]{1,0:T(8,128)(2,1)}), bf16[512,1024]{1,0:T(8,128)(2,1)}) %reduce-scatter.2.cloned.1.call-update) | async-done | bytes 1048592 | tf_op jit(solution)/shard_map/reduce_scatter | solution.py:145
  (91 shorter events, 12.4 us)
Async XLA Ops:
  7.2 5.0 %copy-start = (bf16[512,1024]{1,0:T(8,128)(2,1)S(1)}, bf16[512,1024]{1,0:T(8,128)(2,1)}, u32[]{:S(2)}) copy-start(bf16[512,1024]{1,0:T(8,128)(2,1)} %param.9) | copy-start | bytes 3145732
  7.2 3.0 %copy-start.25 = (s32[512]{0:T(512)S(1)}, s32[512]{0:T(512)}, u32[]{:S(2)}) copy-start(s32[512]{0:T(512)} %param.11) | copy-start | bytes 6148
  7.2 85.9 %all-gather.2.cloned.1.call-start = ((), (), s32[]{:S(2)}) async-start(), calls=%async_computation.2 | async-start | bytes 5242880 | tf_op jit(solution)/shard_map/all_gather | solution.py:90
  7.9 163.3 %reduce-scatter.2.cloned.1.call-start = ((), (), s32[]{:S(2)}) async-start(), calls=%async_computation.1 | async-start | bytes 5242880 | tf_op jit(solution)/shard_map/reduce_scatter | solution.py:145
  9.5 11.6 %copy-start.24 = (f32[8,7,512]{2,0,1:T(8,128)S(1)}, f32[8,7,512]{2,0,1:T(8,128)}, u32[]{:S(2)}) copy-start(f32[8,7,512]{2,0,1:T(8,128)} %param.10) | copy-start | bytes 344068
  10.2 15.2 %copy-start.14 = (bf16[512,8,128]{0,2,1:T(8,128)(2,1)}, bf16[512,8,128]{0,2,1:T(8,128)(2,1)S(1)}, u32[]{:S(2)}) copy-start(bf16[512,8,128]{0,2,1:T(8,128)(2,1)S(1)} %copy.15) | copy-start | bytes 3145732
  12.6 9.8 %copy-start.17 = (f32[8,128,128]{2,1,0:T(8,128)}, f32[8,128,128]{2,1,0:T(8,128)S(1)}, u32[]{:S(2)}) copy-start(f32[8,128,128]{2,1,0:T(8,128)S(1)} %get-tuple-element.27) | copy-start | bytes 1572868
  12.6 4.8 %collective-permute-start.1 = (bf16[8,128,128]{2,1,0:T(8,128)(2,1)S(1)}, bf16[8,128,128]{2,1,0:T(8,128)(2,1)S(1)}, u32[]{:S(2)}, u32[]{:S(2)}) collective-permute-start(bf16[8,128,128]{2,1,0:T(8,128)(2,1)S(1)} %get-tuple-element.26), channel_id=1, source_target_pairs={{0,4},{4,0},{8,12},{12,8},{16,20},{20,16},{24,28},{28,24},{1,5},{5... | collective-permute-start | bytes 786440 | tf_op jit(solution)/shard_map/ppermute | solution.py:12
  13.8 2.9 %collective-permute-start = (bf16[1]{0:T(256)(128)(2,1)}, bf16[1]{0:T(256)(128)(2,1)}, u32[]{:S(2)}, u32[]{:S(2)}) collective-permute-start(bf16[1]{0:T(256)(128)(2,1)} %convert_element_type.180), channel_id=1, source_target_pairs={{0,4},{4,0},{8,12},{12,8},{16,20},{20,16},{24,28},{28,24},{1,5},{5... | collective-permute-start | bytes 14 | tf_op jit(solution)/shard_map/ppermute | solution.py:12
  18.2 13.0 %collective-permute-start.3 = (bf16[8,128,128]{2,1,0:T(8,128)(2,1)}, bf16[8,128,128]{2,1,0:T(8,128)(2,1)}, u32[]{:S(2)}, u32[]{:S(2)}) collective-permute-start(bf16[8,128,128]{2,1,0:T(8,128)(2,1)} %fusion.65), channel_id=1, source_target_pairs={{0,8},{4,12},{8,0},{12,4},{16,24},{20,28},{24,16},{28,20},{1,9},{5... | collective-permute-start | bytes 786440 | tf_op jit(solution)/shard_map/ppermute | solution.py:12
  21.7 13.1 %copy-start.26 = (f32[8,512]{1,0:T(8,128)S(1)}, f32[8,512]{1,0:T(8,128)}, u32[]{:S(2)}) copy-start(f32[8,512]{1,0:T(8,128)} %get-tuple-element.16) | copy-start | bytes 49156
  21.7 13.1 %copy-start.27 = (f32[8,512]{1,0:T(8,128)S(1)}, f32[8,512]{1,0:T(8,128)}, u32[]{:S(2)}) copy-start(f32[8,512]{1,0:T(8,128)} %get-tuple-element.17) | copy-start | bytes 49156
  21.7 13.1 %copy-start.28 = (f32[8,512]{1,0:T(8,128)S(1)}, f32[8,512]{1,0:T(8,128)}, u32[]{:S(2)}) copy-start(f32[8,512]{1,0:T(8,128)} %get-tuple-element.18) | copy-start | bytes 49156
  27.0 3.6 %collective-permute-start.2 = (bf16[1]{0:T(256)(128)(2,1)}, bf16[1]{0:T(256)(128)(2,1)}, u32[]{:S(2)}, u32[]{:S(2)}) collective-permute-start(bf16[1]{0:T(256)(128)(2,1)} %convert_element_type.185), channel_id=1, source_target_pairs={{0,8},{4,12},{8,0},{12,4},{16,24},{20,28},{24,16},{28,20},{1,9},{5... | collective-permute-start | bytes 14 | tf_op jit(solution)/shard_map/ppermute | solution.py:12
  33.3 16.8 %copy-start.4 = (f32[1,8,128,128]{3,2,1,0:T(8,128)}, f32[1,8,128,128]{3,2,1,0:T(8,128)S(1)}, u32[]{:S(2)}) copy-start(f32[1,8,128,128]{3,2,1,0:T(8,128)S(1)} %get-tuple-element.12) | copy-start | bytes 1572868
  33.3 16.8 %copy-start.6 = (f32[1,8,128,128]{3,2,1,0:T(8,128)}, f32[1,8,128,128]{3,2,1,0:T(8,128)S(1)}, u32[]{:S(2)}) copy-start(f32[1,8,128,128]{3,2,1,0:T(8,128)S(1)} %get-tuple-element.14) | copy-start | bytes 1572868
  33.3 15.7 %collective-permute-start.5 = (bf16[8,128,128]{2,1,0:T(8,128)(2,1)}, bf16[8,128,128]{2,1,0:T(8,128)(2,1)S(1)}, u32[]{:S(2)}, u32[]{:S(2)}) collective-permute-start(bf16[8,128,128]{2,1,0:T(8,128)(2,1)} %get-tuple-element.13), channel_id=1, source_target_pairs={{0,16},{4,20},{8,24},{12,28},{16,0},{20,4},{24,8},{28,12},{1,17},{... | collective-permute-start | bytes 786440 | tf_op jit(solution)/shard_map/ppermute | solution.py:12
  44.7 3.6 %collective-permute-start.4 = (bf16[1]{0:T(256)(128)(2,1)}, bf16[1]{0:T(256)(128)(2,1)}, u32[]{:S(2)}, u32[]{:S(2)}) collective-permute-start(bf16[1]{0:T(256)(128)(2,1)} %select_n.196), channel_id=1, source_target_pairs={{0,16},{4,20},{8,24},{12,28},{16,0},{20,4},{24,8},{28,12},{1,17},{... | collective-permute-start | bytes 14 | tf_op jit(solution)/shard_map/ppermute | solution.py:12
  49.0 1.1 copy-start.8
  49.0 5.2 %slice-start = ((s8[8388608]{0:T(1024)(128)(4,1)}), s8[4194304]{0:T(1024)(128)(4,1)S(1)}, s32[]{:S(2)}) async-start(s8[8388608]{0:T(1024)(128)(4,1)} %bitcast.150), calls=%async_computation.3 | async-start | bytes 8388608
  50.1 2.6 %copy-start.1 = (bf16[8,512,512]{2,1,0:T(8,128)(2,1)S(1)}, bf16[8,512,512]{2,1,0:T(8,128)(2,1)}, u32[]{:S(2)}) copy-start(bf16[8,512,512]{2,1,0:T(8,128)(2,1)} %multiply_convert_fusion.2) | copy-start | bytes 12582916
  50.1 4.1 %slice-start.1 = ((s8[8388608]{0:T(1024)(128)(4,1)}), s8[4194304]{0:T(1024)(128)(4,1)S(1)}, s32[]{:S(2)}) async-start(s8[8388608]{0:T(1024)(128)(4,1)} %bitcast.150), calls=%async_computation.4 | async-start | bytes 8388608
  60.7 1.2 collective-permute-start.6
  63.3 3.7 %collective-permute-start.8 = (bf16[1]{0:T(256)(128)(2,1)}, bf16[1]{0:T(256)(128)(2,1)}, u32[]{:S(2)}, u32[]{:S(2)}) collective-permute-start(bf16[1]{0:T(256)(128)(2,1)} %convert_element_type.209), channel_id=1, source_target_pairs={{0,8},{4,12},{8,0},{12,4},{16,24},{20,28},{24,16},{28,20},{1,9},{5... | collective-permute-start | bytes 14 | tf_op jit(solution)/shard_map/ppermute | solution.py:12
  68.2 3.7 %collective-permute-start.10 = (bf16[1]{0:T(256)(128)(2,1)}, bf16[1]{0:T(256)(128)(2,1)}, u32[]{:S(2)}, u32[]{:S(2)}) collective-permute-start(bf16[1]{0:T(256)(128)(2,1)} %select_n.214), channel_id=1, source_target_pairs={{0,16},{4,20},{8,24},{12,28},{16,0},{20,4},{24,8},{28,12},{1,17},{... | collective-permute-start | bytes 14 | tf_op jit(solution)/shard_map/ppermute | solution.py:12
  108.5 2.8 %copy-start.18 = (f32[8,512,128]{1,2,0:T(8,128)S(1)}, f32[8,512,128]{1,2,0:T(8,128)}, u32[]{:S(2)}) copy-start(f32[8,512,128]{1,2,0:T(8,128)} %copy.30) | copy-start | bytes 6291460
  111.3 1.1 copy-start.5
  111.3 1.2 copy-start.7
  111.3 1.3 copy-start.9
  112.3 7.7 %collective-permute-start.7 = (bf16[3,8,128,128]{2,3,0,1:T(8,128)(2,1)S(1)}, bf16[3,8,128,128]{2,3,0,1:T(8,128)(2,1)S(1)}, u32[]{:S(2)}, u32[]{:S(2)}) collective-permute-start(bf16[3,8,128,128]{2,3,0,1:T(8,128)(2,1)S(1)} %get-tuple-element.28), channel_id=1, source_target_pairs={{0,4},{4,0},{8,12},{12,8},{16,20},{20,16},{24,28},{28,24},{1,5},{5... | collective-permute-start | bytes 2359304 | tf_op jit(solution)/shard_map/ppermute | solution.py:12
  112.6 1.2 copy-start.13
  112.6 1.3 copy-start.19
  112.6 1.3 copy-start.20
  112.6 1.4 copy-start.21
  112.6 1.5 copy-start.22
  112.6 1.6 copy-start.23
  120.0 4.6 %copy-start.2 = (bf16[8,512,512]{2,1,0:T(8,128)(2,1)}, bf16[8,512,512]{2,1,0:T(8,128)(2,1)S(1)}, u32[]{:S(2)}) copy-start(bf16[8,512,512]{2,1,0:T(8,128)(2,1)S(1)} %multiply_convert_fusion.1) | copy-start | bytes 12582916
  120.2 1.8 copy-start.12
  122.0 2.6 %copy-start.15 = (bf16[512,8,128]{0,2,1:T(8,128)(2,1)S(1)}, bf16[512,8,128]{0,2,1:T(8,128)(2,1)}, u32[]{:S(2)}) copy-start(bf16[512,8,128]{0,2,1:T(8,128)(2,1)} %copy-done.14) | copy-start | bytes 3145732
  122.0 14.4 %collective-permute-start.9 = (bf16[2,8,128,128]{2,3,0,1:T(8,128)(2,1)}, bf16[2,8,128,128]{2,3,0,1:T(8,128)(2,1)}, u32[]{:S(2)}, u32[]{:S(2)}) collective-permute-start(bf16[2,8,128,128]{2,3,0,1:T(8,128)(2,1)} %get-tuple-element.10), channel_id=1, source_target_pairs={{0,8},{4,12},{8,0},{12,4},{16,24},{20,28},{24,16},{28,20},{1,9},{5... | collective-permute-start | bytes 1572872 | tf_op jit(solution)/shard_map/ppermute | solution.py:12
  138.7 7.7 %collective-permute-start.11 = (bf16[1,8,128,128]{2,3,0,1:T(8,128)(2,1)S(1)}, bf16[1,8,128,128]{2,3,0,1:T(8,128)(2,1)S(1)}, u32[]{:S(2)}, u32[]{:S(2)}) collective-permute-start(bf16[1,8,128,128]{2,3,0,1:T(8,128)(2,1)S(1)} %add_convert_fusion.1), channel_id=1, source_target_pairs={{0,16},{4,20},{8,24},{12,28},{16,0},{20,4},{24,8},{28,12},{1,17},{... | collective-permute-start | bytes 786440 | tf_op jit(solution)/shard_map/ppermute | solution.py:12
  144.5 4.1 %copy-start.3 = (bf16[8,512,512]{2,1,0:T(8,128)(2,1)S(1)}, bf16[8,512,512]{2,1,0:T(8,128)(2,1)}, u32[]{:S(2)}) copy-start(bf16[8,512,512]{2,1,0:T(8,128)(2,1)} %copy-done.2) | copy-start | bytes 12582916
  144.5 4.1 %copy-start.16 = (bf16[512,8,128]{0,2,1:T(8,128)(2,1)S(1)}, bf16[512,8,128]{0,2,1:T(8,128)(2,1)}, u32[]{:S(2)}) copy-start(bf16[512,8,128]{0,2,1:T(8,128)(2,1)} %copy.28) | copy-start | bytes 3145732
  148.6 4.0 %copy-start.10 = (bf16[512,1024]{1,0:T(8,128)(2,1)S(1)}, bf16[512,1024]{1,0:T(8,128)(2,1)}, u32[]{:S(2)}) copy-start(bf16[512,1024]{1,0:T(8,128)(2,1)} %param.8) | copy-start | bytes 3145732
  152.6 1.6 copy-start.11
Sparse Core Ops, SparseCore 0:
  9.6 83.4 all-gather.1
  96.0 75.2 reduce-scatter.1
where the time goes:
time: 179 us; the launch traced here: 178 us
  waiting for transfers between devices  52.9 us (30%)
  matrix products  50.5 us (28%)
  between operations  22.4 us (13%)
  local copies, waits for them, and re-layouts  20.6 us (12%)
  starting transfers between devices  17 us (9%)
  other arithmetic  14.7 us (8%)
    all_gather x1, waiting for transfers between devices, shards(): lax.all_gather(out_grad, 'head', axis=1, tiled=True)  20.5 us
    ppermute x12, waiting for transfers between devices, from_partner(): return lax.ppermute(value, axis, pairs)  18.5 us
    ppermute x12, starting transfers between devices, from_partner(): return lax.ppermute(value, axis, pairs)  16.9 us
    reduce_scatter x1, waiting for transfers between devices, shards(): lax.psum_scatter(partial_value.astype(jnp.bfloat16), 'head', scatter_dime...  13.2 us
    unnamed x68, local copies, waits for them, and re-layouts  12.7 us
    dot_general x1, matrix products, shards(): jnp.einsum('tc,rc->tr', lax.all_gather(out_grad, 'head', axis=1, tiled=Tr...  9.17 us
    dot_general x1, matrix products, shards(): jnp.einsum('thd,shd->hts', query_heads, key_heads, preferred_element_type...  8.4 us
    dot_general x1, matrix products, shards(): jnp.dot(attention, out_weight, preferred_element_type=jnp.float32)  6.39 us
  transfers between devices with their start and end apart: 14, of which 9 were waited for; matrix products, arithmetic and copies ran while one was open for 46% of the time, Pallas kernels for 0%

commit v1 on v0

v1 whole, which is shorter than its diff:
```python
import functools

import jax
import jax.numpy as jnp
from jax import lax
from jax.experimental import pallas as pl
from jax.experimental.pallas import tpu as pltpu
from jax.sharding import PartitionSpec as P

SPAN = 64
F32 = jnp.float32
BF16 = jnp.bfloat16


def mm(a, b, ca=1, cb=0):
    return lax.dot_general(a, b, (((ca,), (cb,)), ((), ())), preferred_element_type=F32)


def table(seg_col, seg_row, rows, near):
    t = lax.broadcasted_iota(jnp.int32, (rows, rows), 0)
    s = lax.broadcasted_iota(jnp.int32, (rows, rows), 1)
    differ = jnp.bitwise_xor(t // SPAN, s // SPAN)
    level = jnp.zeros((rows, rows), jnp.int32)
    for section in range(near - 1):
        level = level + (differ >= 1 << section).astype(jnp.int32)
    return jnp.where((t >= s) & (seg_col == seg_row), level, near)


def near_weight(table_ref, cols, near):
    level = table_ref[...]
    weight = jnp.zeros(level.shape, F32)
    for j in range(near):
        weight = jnp.where(level == j, cols[:, j : j + 1], weight)
    return weight


def summary_kernel(levels, k_ref, v_ref, ext_ref, out_ref):
    cols = ext_ref[0].T
    seg = cols[:, levels : levels + 1]
    keep = (seg == seg[-1:, :]).astype(F32)
    masked = (k_ref[...].astype(F32) * keep).astype(BF16)
    out_ref[0] = mm(masked, v_ref[...], 0, 0).astype(BF16)


def forward_kernel(near, levels, q_ref, k_ref, v_ref, ext_ref, inc_ref, out_ref, table_ref):
    rows = q_ref.shape[0]
    ext = ext_ref[0]
    cols = ext.T

    @pl.when(pl.program_id(0) == 0)
    def _():
        table_ref[...] = table(cols[:, levels : levels + 1], ext[levels : levels + 1], rows, near)

    q = q_ref[...]
    weight = near_weight(table_ref, cols, near)
    probs = (weight * mm(q, k_ref[...], 1, 1)).astype(BF16)
    out = mm(probs, v_ref[...])
    for j in range(levels - near):
        out = out + cols[:, near + j : near + j + 1] * mm(q, inc_ref[j, 0])
    out_ref[...] = out.astype(BF16)


def leaf_kernel(near, levels, q_ref, g_ref, ext_ref, out_ref):
    cols = ext_ref[0].T
    q = q_ref[...]
    g = g_ref[...].astype(F32)
    for j in range(levels - near):
        scaled = (g * cols[:, near + j : near + j + 1]).astype(BF16)
        out_ref[j, 0] = mm(q, scaled, 0, 0).astype(BF16)


def backward_kernel(
    near, levels, q_ref, k_ref, v_ref, g_ref, ext_ref, inc_ref, dq_ref, dk_ref, dv_ref, table_ref
):
    rows = q_ref.shape[0]
    ext = ext_ref[0]
    cols = ext.T

    @pl.when(pl.program_id(0) == 0)
    def _():
        table_ref[...] = table(cols[:, levels : levels + 1], ext[levels : levels + 1], rows, near)

    q, k, v, g = q_ref[...], k_ref[...], v_ref[...], g_ref[...]
    weight = near_weight(table_ref, cols, near)
    probs = (weight * mm(q, k, 1, 1)).astype(BF16)
    dv_ref[...] = mm(probs, g, 0, 0)
    grads = (weight * mm(g, v, 1, 1)).astype(BF16)
    dk_ref[...] = mm(grads, q, 0, 0)
    dq = mm(grads, k)
    for j in range(levels - near):
        dq = dq + cols[:, near + j : near + j + 1] * mm(g, inc_ref[j, 0], 1, 1)
    dq_ref[...] = dq.astype(BF16)


def finish_kernel(levels, k_ref, v_ref, ext_ref, in_ref, ndk_ref, ndv_ref, dk_ref, dv_ref):
    seg = ext_ref[0].T[:, levels : levels + 1]
    keep = (seg == seg[-1:, :]).astype(F32)
    state = in_ref[0]
    dk_ref[...] = (ndk_ref[...] + keep * mm(v_ref[...], state, 1, 1)).astype(BF16)
    dv_ref[...] = (ndv_ref[...] + keep * mm(k_ref[...], state)).astype(BF16)


def head_call(kernel, heads, args, specs, outs, out_specs, flops, scratch=()):
    return pl.pallas_call(
        kernel,
        grid=(heads,),
        in_specs=specs,
        out_specs=out_specs,
        out_shape=outs,
        scratch_shapes=scratch,
        cost_estimate=pl.CostEstimate(flops=flops, bytes_accessed=1 << 22, transcendentals=0),
        compiler_params=pltpu.CompilerParams(vmem_limit_bytes=40 << 20),
    )(*args)


def swap(value, axis, section):
    pairs = [(i, i ^ (1 << section)) for i in range(lax.axis_size(axis))]
    return lax.ppermute(value, axis, pairs)


def shards(queries, keys, values, gates, segment_ids, out_weight, out_grad):
    rows = queries.shape[0]
    heads, levels = gates.shape[0], gates.shape[1]
    dk = queries.shape[1] // heads
    dv = values.shape[1] // heads
    near = (rows // SPAN).bit_length()
    spread = lax.axis_size("ctx").bit_length() - 1
    me = lax.axis_index("ctx")
    z = lax.axis_index("head")
    count = lax.axis_size("head")
    width = out_grad.shape[1]

    ends = jnp.stack([segment_ids[0], segment_ids[rows - 1]]).astype(F32)
    marks = lax.all_gather(ends, "ctx")
    first, last = ends[0], ends[1]

    seg = segment_ids.astype(F32)
    keep_high = (segment_ids == segment_ids[0]).astype(F32)
    size = -(-(levels + 1) // 8) * 8
    ext = jnp.concatenate(
        [
            gates[:, :near],
            gates[:, near:] * keep_high,
            jnp.broadcast_to(seg, (heads, 1, rows)),
            jnp.zeros((heads, size - levels - 1, rows), F32),
        ],
        axis=1,
    )

    kspec = pl.BlockSpec((rows, dk), lambda h: (0, h))
    vspec = pl.BlockSpec((rows, dv), lambda h: (0, h))
    espec = pl.BlockSpec((1, size, rows), lambda h: (h, 0, 0))
    sspec = pl.BlockSpec((1, dk, dv), lambda h: (h, 0, 0))
    ispec = pl.BlockSpec((levels - near, 1, dk, dv), lambda h: (0, h, 0, 0))
    wide = jax.ShapeDtypeStruct((rows, heads * dk), BF16)
    wide_v = jax.ShapeDtypeStruct((rows, heads * dv), BF16)
    scratch = [pltpu.VMEM((rows, rows), jnp.int32)]
    near_flops = 2 * rows * rows * dk * heads

    def product(block, owner):
        part = lax.dynamic_slice_in_dim(out_weight, owner * width, width, 1)
        return mm(block, part, 1, 1)

    going_right = going_left = out_grad
    received = []
    for step in range(count - 1):
        going_right = lax.ppermute(
            going_right, "head", [(i, i + 1) for i in range(step, count - 1)]
        )
        going_left = lax.ppermute(going_left, "head", [(i, i - 1) for i in range(1, count - step)])
        received.append((going_right, going_left))
    total = product(out_grad, z)

    state = head_call(
        functools.partial(summary_kernel, levels),
        heads,
        (keys, values, ext),
        [kspec, vspec, espec],
        jax.ShapeDtypeStruct((heads, dk, dv), BF16),
        sspec,
        2 * rows * dk * dv * heads,
    )
    pieces = []
    for section in range(spread):
        low = (1 << section) - 1
        partner = swap(state, "ctx", section)
        upper = (me >> section) & 1 == 1
        partner_mark = marks[(me ^ (1 << section)) | low, 1]
        own_mark = marks[me | low, 1]
        zero = jnp.zeros((), BF16)
        pieces.append(jnp.where(upper & (partner_mark == first), partner, zero))
        joined = partner_mark == own_mark
        state = jnp.where(upper | joined, state, zero) + jnp.where(upper & ~joined, zero, partner)
    incoming = jnp.stack(pieces)
    attention = head_call(
        functools.partial(forward_kernel, near, levels),
        heads,
        (queries, keys, values, ext, incoming),
        [kspec, kspec, vspec, espec, ispec],
        wide_v,
        vspec,
        3 * near_flops,
        scratch,
    )

    projected = mm(attention, out_weight).astype(BF16)

    def share(owner):
        return lax.dynamic_slice_in_dim(projected, owner * width, width, 1).astype(F32)

    sum_right = sum_left = None
    for step in range(count - 1):
        reach = count - 1 - step
        mine_right = share(jnp.minimum(z + reach, count - 1))
        mine_left = share(jnp.maximum(z - reach, 0))
        if step:
            mine_right = mine_right + sum_right.astype(F32)
            mine_left = mine_left + sum_left.astype(F32)
        sum_right = lax.ppermute(
            mine_right.astype(BF16), "head", [(i, i + 1) for i in range(step + 1)]
        )
        sum_left = lax.ppermute(
            mine_left.astype(BF16), "head", [(i, i - 1) for i in range(reach, count)]
        )
    mixed = (share(z) + sum_right.astype(F32) + sum_left.astype(F32)).astype(BF16)

    for step, (right, left) in enumerate(received):
        if step == count - 2:
            end = z == count - 1
            total = total + product(
                jnp.where(end, right, left), jnp.where(end, 0, count - 1)
            )
        else:
            total = total + product(right, jnp.maximum(z - step - 1, 0))
            total = total + product(left, jnp.minimum(z + step + 1, count - 1))
    cot = total.astype(BF16)

    dual = head_call(
        functools.partial(leaf_kernel, near, levels),
        heads,
        (queries, cot, ext),
        [kspec, vspec, espec],
        jax.ShapeDtypeStruct((levels - near, heads, dk, dv), BF16),
        ispec,
        2 * rows * dk * dv * heads * (levels - near),
    )
    inbound = jnp.zeros((heads, dk, dv), F32)
    for section in range(spread):
        low = (1 << section) - 1
        partner = swap(dual, "ctx", section)
        upper = (me >> section) & 1 == 1
        partner_mark = marks[(me ^ (1 << section)) & ~low, 0]
        own_mark = marks[me & ~low, 0]
        zero = jnp.zeros((), BF16)
        inbound = inbound + jnp.where(~upper & (partner_mark == last), partner[0], zero).astype(F32)
        joined = partner_mark == own_mark
        dual = jnp.where(upper & ~joined, zero, dual[1:]) + jnp.where(
            upper | joined, partner[1:], zero
        )
    near_dk = jax.ShapeDtypeStruct((rows, heads * dk), F32)
    near_dv = jax.ShapeDtypeStruct((rows, heads * dv), F32)
    grad_queries, near_dk, near_dv = head_call(
        functools.partial(backward_kernel, near, levels),
        heads,
        (queries, keys, values, cot, ext, incoming),
        [kspec, kspec, vspec, vspec, espec, ispec],
        (wide, near_dk, near_dv),
        (kspec, kspec, vspec),
        6 * near_flops,
        scratch,
    )
    grad_keys, grad_values = head_call(
        functools.partial(finish_kernel, levels),
        heads,
        (keys, values, ext, inbound.astype(BF16), near_dk, near_dv),
        [kspec, vspec, espec, sspec, kspec, vspec],
        (wide, wide_v),
        (kspec, vspec),
        4 * rows * dk * dv * heads,
    )
    return (mixed, grad_queries, grad_keys, grad_values)


def solution(mesh):
    placed = (
        P("ctx", "head"),
        P("ctx", "head"),
        P("ctx", "head"),
        P("head", None, "ctx"),
        P("ctx"),
        P("head", None),
        P("ctx", "head"),
    )
    return jax.shard_map(
        shards,
        mesh=mesh,
        in_specs=placed,
        out_specs=(P("ctx", "head"), P("ctx", "head"), P("ctx", "head"), P("ctx", "head")),
        check_vma=False,
    )
```

time: 179 us -> 201 us (1.12)
  the two profiles are of different devices: /device:TPU:0 before, /device:TPU:16 now
where the time goes in v1:
time: 201 us; the launch traced here: 199 us
  Pallas kernels  43.8 us (22%)
  waiting for transfers between devices  41 us (20%)
  starting transfers between devices  32.9 us (16%)
  other arithmetic  24.2 us (12%)
  matrix products  23.8 us (12%)
  between operations  13.5 us (7%)
  local copies, waits for them, and re-layouts  11.5 us (6%)
  blocking collectives  8.74 us (4%)
    pallas_call x5, Pallas kernels, head_call(): pl.pallas_call(kernel, grid=(heads,), in_specs=specs, out_specs=out_specs...  43.8 us
    dot_general x7, matrix products, mm(): lax.dot_general(a, b, (((ca,), (cb,)), ((), ())), preferred_element_type=...  23.8 us
    ppermute x3, waiting for transfers between devices, shards(): lax.ppermute(mine_left.astype(BF16), 'head', [(i, i - 1) for i in range(r...  13.2 us
    ppermute x3, waiting for transfers between devices, shards(): lax.ppermute(going_right, 'head', [(i, i + 1) for i in range(step, count...  13.1 us
    all_gather x1, blocking collectives, shards(): marks = lax.all_gather(ends, 'ctx')  8.74 us
    ppermute x3, starting transfers between devices, shards(): lax.ppermute(going_right, 'head', [(i, i + 1) for i in range(step, count...  8.65 us
    ppermute x3, starting transfers between devices, shards(): lax.ppermute(mine_left.astype(BF16), 'head', [(i, i - 1) for i in range(r...  8.56 us
    ppermute x3, waiting for transfers between devices, shards(): lax.ppermute(mine_right.astype(BF16), 'head', [(i, i + 1) for i in range(...  8.36 us
  transfers between devices with their start and end apart: 18, of which 5 were waited for; matrix products, arithmetic and copies ran while one was open for 22% of the time, Pallas kernels for 20%

profile of v1, /device:TPU:16, one launch (start us, length us, event | category | flops | bytes accessed | tf_op | source)
XLA Modules:
  0.0 199.4 jit_solution(1172244537297159504)
XLA Ops:
  2.3 1.3 fusion.27
  4.3 1.3 compare_convert_fusion
  5.8 1.2 copy-done
  7.0 1.2 copy-done.2
  8.3 4.2 %shard_map.102 = bf16[8,128,128]{2,1,0:T(8,128)(2,1)S(1)} custom-call(bf16[512,1024]{1,0:T(8,128)(2,1)S(1)} %copy-done, bf16[512,1024]{1,0:T(8,128)(2,1)S(1)} %copy-done.2, f32[8,8,512]{2,1,0:T(8,128)S(1)} %pad_maximum_fusion.1.ext_ref), custom_call_target="tpu_custom_call" | custom-call | flops 134217728 | bytes 4194304 | tf_op jit(solution)/shard_map/pallas_call | solution.py:104
  12.5 1.4 fusion.26
  13.9 8.7 %all-gather = f32[8,1,2]{2,1,0:T(1,128)S(1)} all-gather(f32[1,1,2]{2,1,0:T(1,128)S(1)} %fusion.26), channel_id=1, replica_groups=mesh['ctx'=8,'head'=4] {'ctx'}, dimensions={0}, use_global_device_ids=true | all-gather | bytes 72 | tf_op jit(solution)/shard_map/all_gather | solution.py:134
  24.6 1.4 add_convert_fusion.7
  27.8 1.9 select_bitcast_fusion.2
  29.8 1.5 collective-permute-start.1
  31.3 2.3 %collective-permute-start.10 = (bf16[512,1024]{1,0:T(8,128)(2,1)}, bf16[512,1024]{1,0:T(8,128)(2,1)}, u32[]{:S(2)}, u32[]{:S(2)}) collective-permute-start(bf16[512,1024]{1,0:T(8,128)(2,1)} %param.13), channel_id=1, source_target_pairs={{1,0},{2,1},{3,2},{5,4},{6,5},{7,6},{9,8},{10,9},{11,10},{13,12},{... | collective-permute-start | bytes 3145736 | tf_op jit(solution)/shard_map/ppermute | solution.py:170
  33.6 4.5 %collective-permute-start.9 = (bf16[512,1024]{1,0:T(8,128)(2,1)}, bf16[512,1024]{1,0:T(8,128)(2,1)}, u32[]{:S(2)}, u32[]{:S(2)}) collective-permute-start(bf16[512,1024]{1,0:T(8,128)(2,1)} %param.13), channel_id=1, source_target_pairs={{0,1},{1,2},{2,3},{4,5},{5,6},{6,7},{8,9},{9,10},{10,11},{12,13},{... | collective-permute-start | bytes 3145736 | tf_op jit(solution)/shard_map/ppermute | solution.py:167
  40.6 1.8 select_bitcast_fusion.1
  44.0 6.4 %collective-permute-done.2 = bf16[8,128,128]{2,1,0:T(8,128)(2,1)} collective-permute-done((bf16[8,128,128]{2,1,0:T(8,128)(2,1)}, bf16[8,128,128]{2,1,0:T(8,128)(2,1)}, u32[]{:S(2)}, u32[]{:S(2)}) %collective-permute-start.2) | collective-permute-done | bytes 262176 | tf_op jit(solution)/shard_map/ppermute | solution.py:118
  51.5 11.6 %shard_map.103 = bf16[512,1024]{1,0:T(8,128)(2,1)S(1)} custom-call(bf16[512,1024]{1,0:T(8,128)(2,1)S(1)} %copy-done.4, bf16[512,1024]{1,0:T(8,128)(2,1)S(1)} %copy-done.1, bf16[512,1024]{1,0:T(8,128)(2,1)S(1)} %copy-done.3, f32[8,8,512]{2,1,0:T(8,128)S(1)} %pad_maximum_fusion.1.ext_ref, bf16[3,8,128,128]{3,2,1,0:T(8,128)(2,1)S(1)} %pad_maximum_fusion.inc_ref), custom_call_target="tpu_custom_call" | custom-call | flops 1610612736 | bytes 4194304 | tf_op jit(solution)/shard_map/pallas_call | solution.py:104
  63.1 2.3 %collective-permute-start.12 = (bf16[512,1024]{1,0:T(8,128)(2,1)}, bf16[512,1024]{1,0:T(8,128)(2,1)}, u32[]{:S(2)}, u32[]{:S(2)}) collective-permute-start(bf16[512,1024]{1,0:T(8,128)(2,1)} %collective-permute-done.10), channel_id=1, source_target_pairs={{1,0},{2,1},{5,4},{6,5},{9,8},{10,9},{13,12},{14,13},{17,16},{18,1... | collective-permute-start | bytes 3145736 | tf_op jit(solution)/shard_map/ppermute | solution.py:170
  65.4 1.9 collective-permute-start.11
  67.3 8.1 %convolution_convert_fusion = bf16[512,4096]{1,0:T(8,128)(2,1)S(1)} fusion(bf16[512,1024]{1,0:T(8,128)(2,1)S(1)} %shard_map.103, bf16[1024,4096]{1,0:T(8,128)(2,1)} %param.12), kind=kOutput, calls=%fused_computation | convolution fusion | flops 4297064448 | bytes 13631488 | tf_op jit(solution)/shard_map/dot_general | solution.py:16
  75.4 1.3 constant_dynamic-slice_fusion.11
  77.7 1.6 collective-permute-start.3
  79.4 3.3 %fusion.11 = f32[1024,512]{0,1:T(8,128)S(1)} fusion(bf16[512,1024]{1,0:T(8,128)(2,1)} %param.13, bf16[1024,4096]{1,0:T(8,128)(2,1)} %param.12, s32[]{:T(128)S(6)} %select_n.185), kind=kOutput, calls=%fused_computation.13 | convolution fusion | flops 1073741824 | bytes 5242884 | tf_op jit(solution)/shard_map/dot_general | solution.py:16
  82.7 1.6 collective-permute-start.6
  84.3 3.2 %fusion.7 = f32[1024,512]{0,1:T(8,128)S(1)} fusion(bf16[512,1024]{1,0:T(8,128)(2,1)} %collective-permute-done.10, bf16[1024,4096]{1,0:T(8,128)(2,1)} %param.12, s32[]{:T(128)S(6)} %select_n.186), kind=kOutput, calls=%fused_computation.9 | convolution fusion | flops 1073741824 | bytes 5242884 | tf_op jit(solution)/shard_map/dot_general | solution.py:16
  87.4 3.7 %collective-permute-done.11 = bf16[512,1024]{1,0:T(8,128)(2,1)} collective-permute-done((bf16[512,1024]{1,0:T(8,128)(2,1)}, bf16[512,1024]{1,0:T(8,128)(2,1)}, u32[]{:S(2)}, u32[]{:S(2)}) %collective-permute-start.11) | collective-permute-done | bytes 1048608 | tf_op jit(solution)/shard_map/ppermute | solution.py:167
  91.2 2.3 %collective-permute-start.13 = (bf16[512,1024]{1,0:T(8,128)(2,1)}, bf16[512,1024]{1,0:T(8,128)(2,1)S(1)}, u32[]{:S(2)}, u32[]{:S(2)}) collective-permute-start(bf16[512,1024]{1,0:T(8,128)(2,1)} %collective-permute-done.11), channel_id=1, source_target_pairs={{2,3},{6,7},{10,11},{14,15},{18,19},{22,23},{26,27},{30,31}} | collective-permute-start | bytes 3145736 | tf_op jit(solution)/shard_map/ppermute | solution.py:167
  94.2 2.5 %fusion.9 = f32[1024,512]{0,1:T(8,128)S(1)} fusion(bf16[512,1024]{1,0:T(8,128)(2,1)} %collective-permute-done.9, bf16[1024,4096]{1,0:T(8,128)(2,1)S(1)} %bitcast.37, s32[]{:T(128)S(6)} %select_n.189), kind=kOutput, calls=%fused_computation.11 | convolution fusion | flops 1073741824 | bytes 5242884 | tf_op jit(solution)/shard_map/dot_general | solution.py:16
  96.7 1.6 add_convert_fusion.4
  98.4 1.5 collective-permute-start.4
  99.9 2.5 %fusion.3 = f32[1024,512]{0,1:T(8,128)S(1)} fusion(bf16[512,1024]{1,0:T(8,128)(2,1)} %collective-permute-done.12, bf16[1024,4096]{1,0:T(8,128)(2,1)S(1)} %bitcast.37, s32[]{:T(128)S(6)} %select_n.187), kind=kOutput, calls=%fused_computation.5 | convolution fusion | flops 1073741824 | bytes 5242884 | tf_op jit(solution)/shard_map/dot_general | solution.py:16
  102.4 2.5 %fusion.5 = f32[1024,512]{0,1:T(8,128)S(1)} fusion(bf16[512,1024]{1,0:T(8,128)(2,1)} %collective-permute-done.11, bf16[1024,4096]{1,0:T(8,128)(2,1)S(1)} %bitcast.37, s32[]{:T(128)S(6)} %select_n.190), kind=kOutput, calls=%fused_computation.7 | convolution fusion | flops 1073741824 | bytes 5242884 | tf_op jit(solution)/shard_map/dot_general | solution.py:16
  104.9 9.3 %collective-permute-done.13 = bf16[512,1024]{1,0:T(8,128)(2,1)S(1)} collective-permute-done((bf16[512,1024]{1,0:T(8,128)(2,1)}, bf16[512,1024]{1,0:T(8,128)(2,1)S(1)}, u32[]{:S(2)}, u32[]{:S(2)}) %collective-permute-start.13) | collective-permute-done | bytes 1048608 | tf_op jit(solution)/shard_map/ppermute | solution.py:167
  114.2 1.7 fusion.g_ref
  115.9 6.0 %shard_map.105 = bf16[3,8,128,128]{3,2,1,0:T(8,128)(2,1)} custom-call(bf16[512,1024]{1,0:T(8,128)(2,1)S(1)} %copy-done.5, bf16[512,1024]{1,0:T(8,128)(2,1)S(1)} %fusion.g_ref, f32[8,8,512]{2,1,0:T(8,128)S(1)} %pad_maximum_fusion.1.ext_ref), custom_call_target="tpu_custom_call" | custom-call | flops 402653184 | bytes 4194304 | tf_op jit(solution)/shard_map/pallas_call | solution.py:104
  121.9 8.4 %collective-permute-done.4 = bf16[512,1024]{1,0:T(8,128)(2,1)S(1)} collective-permute-done((bf16[512,1024]{1,0:T(8,128)(2,1)S(1)}, bf16[512,1024]{1,0:T(8,128)(2,1)S(1)}, u32[]{:S(2)}, u32[]{:S(2)}) %collective-permute-start.4) | collective-permute-done | bytes 1048608 | tf_op jit(solution)/shard_map/ppermute | solution.py:219
  130.2 2.3 %add_convert_fusion.3 = (bf16[512,1024]{1,0:T(8,128)(2,1)}, bf16[512,1024]{1,0:T(8,128)(2,1)}) fusion(bf16[512,1024]{1,0:T(8,128)(2,1)S(1)} %collective-permute-done.4, bf16[512,4096]{1,0:T(8,128)(2,1)S(1)} %copy-done.10, s32[]{:T(128)S(6)} %select_n.186, bf16[512,1024]{1,0:T(8,128)(2,1)S(1)} %collective-permute-done.6, s32[]{:T(128)S(6)} %select_n.190), kind=kLoop, calls=%fused_computation.18 | loop fusion | flops 4194304 | bytes 6291464 | tf_op jit(solution)/shard_map/convert_element_type | solution.py:220
  132.5 3.6 %collective-permute-start.7 = (bf16[512,1024]{1,0:T(8,128)(2,1)}, bf16[512,1024]{1,0:T(8,128)(2,1)}, u32[]{:S(2)}, u32[]{:S(2)}) collective-permute-start(bf16[512,1024]{1,0:T(8,128)(2,1)} %get-tuple-element.15), channel_id=1, source_target_pairs={{2,1},{3,2},{6,5},{7,6},{10,9},{11,10},{14,13},{15,14},{18,17},{19... | collective-permute-start | bytes 3145736 | tf_op jit(solution)/shard_map/ppermute | solution.py:222
  137.5 2.1 %fusion.17 = bf16[2,8,128,128]{3,2,1,0:T(8,128)(2,1)} fusion(bf16[3,8,128,128]{3,2,1,0:T(8,128)(2,1)} %collective-permute-done.15, bf16[3,8,128,128]{3,2,1,0:T(8,128)(2,1)} %shard_map.105, pred[]{:T(512)S(6)} %or.26, pred[]{:T(512)S(6)} %and.64), kind=kLoop, calls=%fused_computation.24 | loop fusion | flops 786432 | bytes 1572866 | tf_op jit(solution)/shard_map/add | solution.py:257
  140.0 3.2 %collective-permute-start.5 = (bf16[512,1024]{1,0:T(8,128)(2,1)}, bf16[512,1024]{1,0:T(8,128)(2,1)}, u32[]{:S(2)}, u32[]{:S(2)}) collective-permute-start(bf16[512,1024]{1,0:T(8,128)(2,1)} %get-tuple-element.14), channel_id=1, source_target_pairs={{0,1},{1,2},{2,3},{4,5},{5,6},{6,7},{8,9},{9,10},{10,11},{12,13},{... | collective-permute-start | bytes 3145736 | tf_op jit(solution)/shard_map/ppermute | solution.py:219
  143.2 13.2 %collective-permute-done.7 = bf16[512,1024]{1,0:T(8,128)(2,1)} collective-permute-done((bf16[512,1024]{1,0:T(8,128)(2,1)}, bf16[512,1024]{1,0:T(8,128)(2,1)}, u32[]{:S(2)}, u32[]{:S(2)}) %collective-permute-start.7) | collective-permute-done | bytes 1048608 | tf_op jit(solution)/shard_map/ppermute | solution.py:222
  156.4 2.9 %add_convert_fusion.1 = bf16[512,1024]{1,0:T(8,128)(2,1)} fusion(bf16[512,1024]{1,0:T(8,128)(2,1)} %collective-permute-done.7, bf16[512,4096]{1,0:T(8,128)(2,1)} %copy-done.9, s32[]{:T(128)S(6)} %select_n.189), kind=kLoop, calls=%fused_computation.16 | loop fusion | flops 2097152 | bytes 3145732 | tf_op jit(solution)/shard_map/convert_element_type | solution.py:223
  159.3 3.4 %collective-permute-start.8 = (bf16[512,1024]{1,0:T(8,128)(2,1)}, bf16[512,1024]{1,0:T(8,128)(2,1)}, u32[]{:S(2)}, u32[]{:S(2)}) collective-permute-start(bf16[512,1024]{1,0:T(8,128)(2,1)} %add_convert_fusion.1), channel_id=1, source_target_pairs={{1,0},{2,1},{3,2},{5,4},{6,5},{7,6},{9,8},{10,9},{11,10},{13,12},{... | collective-permute-start | bytes 3145736 | tf_op jit(solution)/shard_map/ppermute | solution.py:222
  168.8 1.5 collective-permute-start.17
  170.3 1.2 copy-done.6
  171.5 1.1 copy-done.8
  172.7 16.8 %shard_map.104 = (bf16[512,1024]{1,0:T(8,128)(2,1)}, f32[512,1024]{1,0:T(8,128)S(1)}, f32[512,1024]{1,0:T(8,128)S(1)}) custom-call(bf16[512,1024]{1,0:T(8,128)(2,1)S(1)} %copy-done.6, bf16[512,1024]{1,0:T(8,128)(2,1)S(1)} %copy-done.1, bf16[512,1024]{1,0:T(8,128)(2,1)S(1)} %copy-done.3, bf16[512,1024]{1,0:T(8,128)(2,1)S(1)} %fusion.g_ref, ...), custom_call_target="tpu_custom_call" | custom-call | flops 3221225472 | bytes 4194304 | tf_op jit(solution)/shard_map/pallas_call | solution.py:104
  189.5 1.2 fusion.18.in_ref
  190.7 5.2 %shard_map.106 = (bf16[512,1024]{1,0:T(8,128)(2,1)}, bf16[512,1024]{1,0:T(8,128)(2,1)}) custom-call(bf16[512,1024]{1,0:T(8,128)(2,1)S(1)} %copy-done.1, bf16[512,1024]{1,0:T(8,128)(2,1)S(1)} %copy-done.3, f32[8,8,512]{2,1,0:T(8,128)S(1)} %pad_maximum_fusion.1.ext_ref, bf16[8,128,128]{2,1,0:T(8,128)(2,1)S(1)} %fusion.18.in_ref, ...), custom_call_target="tpu_custom_call" | custom-call | flops 268435456 | bytes 4194304 | tf_op jit(solution)/shard_map/pallas_call | solution.py:104
  195.9 3.5 %add_convert_fusion = bf16[512,1024]{1,0:T(8,128)(2,1)} fusion(bf16[512,1024]{1,0:T(8,128)(2,1)} %collective-permute-done.8, bf16[512,1024]{1,0:T(8,128)(2,1)} %collective-permute-done.5, bf16[512,4096]{1,0:T(8,128)(2,1)} %copy-done.9, s32[]{:T(128)S(6)} %select_n.185), kind=kLoop, calls=%fused_computation.15 | loop fusion | flops 3145728 | bytes 4194308 | tf_op jit(solution)/shard_map/convert_element_type | solution.py:225
  (53 shorter events, 8.8 us)
Async XLA Ops:
  5.8 1.2 copy-start
  7.0 1.2 copy-start.2
  12.5 15.4 %collective-permute-start = (bf16[8,128,128]{2,1,0:T(8,128)(2,1)S(1)}, bf16[8,128,128]{2,1,0:T(8,128)(2,1)}, u32[]{:S(2)}, u32[]{:S(2)}) collective-permute-start(bf16[8,128,128]{2,1,0:T(8,128)(2,1)S(1)} %shard_map.102), channel_id=1, source_target_pairs={{0,4},{4,0},{8,12},{12,8},{16,20},{20,16},{24,28},{28,24},{1,5},{5... | collective-permute-start | bytes 786440 | tf_op jit(solution)/shard_map/ppermute | solution.py:118
  27.8 23.7 %copy-start.1 = (bf16[512,1024]{1,0:T(8,128)(2,1)S(1)}, bf16[512,1024]{1,0:T(8,128)(2,1)}, u32[]{:S(2)}) copy-start(bf16[512,1024]{1,0:T(8,128)(2,1)} %k_ref.7) | copy-start | bytes 3145732
  27.8 23.7 %copy-start.3 = (bf16[512,1024]{1,0:T(8,128)(2,1)S(1)}, bf16[512,1024]{1,0:T(8,128)(2,1)}, u32[]{:S(2)}) copy-start(bf16[512,1024]{1,0:T(8,128)(2,1)} %v_ref.7) | copy-start | bytes 3145732
  27.8 23.7 %copy-start.4 = (bf16[512,1024]{1,0:T(8,128)(2,1)S(1)}, bf16[512,1024]{1,0:T(8,128)(2,1)}, u32[]{:S(2)}) copy-start(bf16[512,1024]{1,0:T(8,128)(2,1)} %q_ref.5) | copy-start | bytes 3145732
  29.8 10.8 %collective-permute-start.1 = (bf16[8,128,128]{2,1,0:T(8,128)(2,1)}, bf16[8,128,128]{2,1,0:T(8,128)(2,1)}, u32[]{:S(2)}, u32[]{:S(2)}) collective-permute-start(bf16[8,128,128]{2,1,0:T(8,128)(2,1)} %get-tuple-element.19), channel_id=1, source_target_pairs={{0,8},{4,12},{8,0},{12,4},{16,24},{20,28},{24,16},{28,20},{1,9},{5... | collective-permute-start | bytes 786440 | tf_op jit(solution)/shard_map/ppermute | solution.py:118
  31.3 31.8 %collective-permute-start.10 = (bf16[512,1024]{1,0:T(8,128)(2,1)}, bf16[512,1024]{1,0:T(8,128)(2,1)}, u32[]{:S(2)}, u32[]{:S(2)}) collective-permute-start(bf16[512,1024]{1,0:T(8,128)(2,1)} %param.13), channel_id=1, source_target_pairs={{1,0},{2,1},{3,2},{5,4},{6,5},{7,6},{9,8},{10,9},{11,10},{13,12},{... | collective-permute-start | bytes 3145736 | tf_op jit(solution)/shard_map/ppermute | solution.py:170
  33.6 31.8 %collective-permute-start.9 = (bf16[512,1024]{1,0:T(8,128)(2,1)}, bf16[512,1024]{1,0:T(8,128)(2,1)}, u32[]{:S(2)}, u32[]{:S(2)}) collective-permute-start(bf16[512,1024]{1,0:T(8,128)(2,1)} %param.13), channel_id=1, source_target_pairs={{0,1},{1,2},{2,3},{4,5},{5,6},{6,7},{8,9},{9,10},{10,11},{12,13},{... | collective-permute-start | bytes 3145736 | tf_op jit(solution)/shard_map/ppermute | solution.py:167
  42.4 8.0 %collective-permute-start.2 = (bf16[8,128,128]{2,1,0:T(8,128)(2,1)}, bf16[8,128,128]{2,1,0:T(8,128)(2,1)}, u32[]{:S(2)}, u32[]{:S(2)}) collective-permute-start(bf16[8,128,128]{2,1,0:T(8,128)(2,1)} %get-tuple-element.21), channel_id=1, source_target_pairs={{0,16},{4,20},{8,24},{12,28},{16,0},{20,4},{24,8},{28,12},{1,17},{... | collective-permute-start | bytes 786440 | tf_op jit(solution)/shard_map/ppermute | solution.py:118
  51.5 11.6 %copy-start.7 = (bf16[3,8,128,128]{3,2,1,0:T(8,128)(2,1)}, bf16[3,8,128,128]{3,2,1,0:T(8,128)(2,1)S(1)}, u32[]{:S(2)}) copy-start(bf16[3,8,128,128]{3,2,1,0:T(8,128)(2,1)S(1)} %pad_maximum_fusion.inc_ref) | copy-start | bytes 2359300
  63.1 30.3 %collective-permute-start.12 = (bf16[512,1024]{1,0:T(8,128)(2,1)}, bf16[512,1024]{1,0:T(8,128)(2,1)}, u32[]{:S(2)}, u32[]{:S(2)}) collective-permute-start(bf16[512,1024]{1,0:T(8,128)(2,1)} %collective-permute-done.10), channel_id=1, source_target_pairs={{1,0},{2,1},{5,4},{6,5},{9,8},{10,9},{13,12},{14,13},{17,16},{18,1... | collective-permute-start | bytes 3145736 | tf_op jit(solution)/shard_map/ppermute | solution.py:170
  65.4 25.8 %collective-permute-start.11 = (bf16[512,1024]{1,0:T(8,128)(2,1)}, bf16[512,1024]{1,0:T(8,128)(2,1)}, u32[]{:S(2)}, u32[]{:S(2)}) collective-permute-start(bf16[512,1024]{1,0:T(8,128)(2,1)} %collective-permute-done.9), channel_id=1, source_target_pairs={{1,2},{2,3},{5,6},{6,7},{9,10},{10,11},{13,14},{14,15},{17,18},{18... | collective-permute-start | bytes 3145736 | tf_op jit(solution)/shard_map/ppermute | solution.py:167
  75.4 2.3 %copy-start.9 = (bf16[512,4096]{1,0:T(8,128)(2,1)}, bf16[512,4096]{1,0:T(8,128)(2,1)S(1)}, u32[]{:S(2)}) copy-start(bf16[512,4096]{1,0:T(8,128)(2,1)S(1)} %convolution_convert_fusion) | copy-start | bytes 12582916
  77.7 19.0 %collective-permute-start.3 = (bf16[512,1024]{1,0:T(8,128)(2,1)S(1)}, bf16[512,1024]{1,0:T(8,128)(2,1)}, u32[]{:S(2)}, u32[]{:S(2)}) collective-permute-start(bf16[512,1024]{1,0:T(8,128)(2,1)S(1)} %get-tuple-element.16), channel_id=1, source_target_pairs={{0,1},{4,5},{8,9},{12,13},{16,17},{20,21},{24,25},{28,29}} | collective-permute-start | bytes 3145736 | tf_op jit(solution)/shard_map/ppermute | solution.py:219
  79.4 14.8 %slice-start = ((s8[8388608]{0:T(1024)(128)(4,1)}), s8[4194304]{0:T(1024)(128)(4,1)S(1)}, s32[]{:S(2)}) async-start(s8[8388608]{0:T(1024)(128)(4,1)} %bitcast.36), calls=%async_computation | async-start | bytes 8388608
  82.7 11.5 %slice-start.1 = ((s8[8388608]{0:T(1024)(128)(4,1)}), s8[4194304]{0:T(1024)(128)(4,1)S(1)}, s32[]{:S(2)}) async-start(s8[8388608]{0:T(1024)(128)(4,1)} %bitcast.36), calls=%async_computation.1 | async-start | bytes 8388608
  82.7 39.2 %collective-permute-start.6 = (bf16[512,1024]{1,0:T(8,128)(2,1)}, bf16[512,1024]{1,0:T(8,128)(2,1)S(1)}, u32[]{:S(2)}, u32[]{:S(2)}) collective-permute-start(bf16[512,1024]{1,0:T(8,128)(2,1)} %get-tuple-element.17), channel_id=1, source_target_pairs={{3,2},{7,6},{11,10},{15,14},{19,18},{23,22},{27,26},{31,30}} | collective-permute-start | bytes 3145736 | tf_op jit(solution)/shard_map/ppermute | solution.py:222
  87.4 9.3 %copy-start.10 = (bf16[512,4096]{1,0:T(8,128)(2,1)S(1)}, bf16[512,4096]{1,0:T(8,128)(2,1)}, u32[]{:S(2)}) copy-start(bf16[512,4096]{1,0:T(8,128)(2,1)} %copy-done.9) | copy-start | bytes 12582916
  91.2 23.1 %collective-permute-start.13 = (bf16[512,1024]{1,0:T(8,128)(2,1)}, bf16[512,1024]{1,0:T(8,128)(2,1)S(1)}, u32[]{:S(2)}, u32[]{:S(2)}) collective-permute-start(bf16[512,1024]{1,0:T(8,128)(2,1)} %collective-permute-done.11), channel_id=1, source_target_pairs={{2,3},{6,7},{10,11},{14,15},{18,19},{22,23},{26,27},{30,31}} | collective-permute-start | bytes 3145736 | tf_op jit(solution)/shard_map/ppermute | solution.py:167
  93.4 20.8 %collective-permute-start.14 = (bf16[512,1024]{1,0:T(8,128)(2,1)}, bf16[512,1024]{1,0:T(8,128)(2,1)S(1)}, u32[]{:S(2)}, u32[]{:S(2)}) collective-permute-start(bf16[512,1024]{1,0:T(8,128)(2,1)} %collective-permute-done.12), channel_id=1, source_target_pairs={{1,0},{5,4},{9,8},{13,12},{17,16},{21,20},{25,24},{29,28}} | collective-permute-start | bytes 3145736 | tf_op jit(solution)/shard_map/ppermute | solution.py:170
  98.4 31.8 %collective-permute-start.4 = (bf16[512,1024]{1,0:T(8,128)(2,1)S(1)}, bf16[512,1024]{1,0:T(8,128)(2,1)S(1)}, u32[]{:S(2)}, u32[]{:S(2)}) collective-permute-start(bf16[512,1024]{1,0:T(8,128)(2,1)S(1)} %add_convert_fusion.4), channel_id=1, source_target_pairs={{0,1},{1,2},{4,5},{5,6},{8,9},{9,10},{12,13},{13,14},{16,17},{17,1... | collective-permute-start | bytes 3145736 | tf_op jit(solution)/shard_map/ppermute | solution.py:219
  104.9 11.0 %copy-start.5 = (bf16[512,1024]{1,0:T(8,128)(2,1)S(1)}, bf16[512,1024]{1,0:T(8,128)(2,1)}, u32[]{:S(2)}) copy-start(bf16[512,1024]{1,0:T(8,128)(2,1)} %q_ref.5) | copy-start | bytes 3145732
  121.9 15.6 %collective-permute-start.15 = (bf16[3,8,128,128]{3,2,1,0:T(8,128)(2,1)}, bf16[3,8,128,128]{3,2,1,0:T(8,128)(2,1)}, u32[]{:S(2)}, u32[]{:S(2)}) collective-permute-start(bf16[3,8,128,128]{3,2,1,0:T(8,128)(2,1)} %shard_map.105), channel_id=1, source_target_pairs={{0,4},{4,0},{8,12},{12,8},{16,20},{20,16},{24,28},{28,24},{1,5},{5... | collective-permute-start | bytes 2359304 | tf_op jit(solution)/shard_map/ppermute | solution.py:118
  132.5 23.9 %collective-permute-start.7 = (bf16[512,1024]{1,0:T(8,128)(2,1)}, bf16[512,1024]{1,0:T(8,128)(2,1)}, u32[]{:S(2)}, u32[]{:S(2)}) collective-permute-start(bf16[512,1024]{1,0:T(8,128)(2,1)} %get-tuple-element.15), channel_id=1, source_target_pairs={{2,1},{3,2},{6,5},{7,6},{10,9},{11,10},{14,13},{15,14},{18,17},{19... | collective-permute-start | bytes 3145736 | tf_op jit(solution)/shard_map/ppermute | solution.py:222
  139.5 28.2 %collective-permute-start.16 = (bf16[2,8,128,128]{3,2,1,0:T(8,128)(2,1)}, bf16[2,8,128,128]{3,2,1,0:T(8,128)(2,1)}, u32[]{:S(2)}, u32[]{:S(2)}) collective-permute-start(bf16[2,8,128,128]{3,2,1,0:T(8,128)(2,1)} %fusion.17), channel_id=1, source_target_pairs={{0,8},{4,12},{8,0},{12,4},{16,24},{20,28},{24,16},{28,20},{1,9},{5... | collective-permute-start | bytes 1572872 | tf_op jit(solution)/shard_map/ppermute | solution.py:118
  140.0 55.9 %collective-permute-start.5 = (bf16[512,1024]{1,0:T(8,128)(2,1)}, bf16[512,1024]{1,0:T(8,128)(2,1)}, u32[]{:S(2)}, u32[]{:S(2)}) collective-permute-start(bf16[512,1024]{1,0:T(8,128)(2,1)} %get-tuple-element.14), channel_id=1, source_target_pairs={{0,1},{1,2},{2,3},{4,5},{5,6},{6,7},{8,9},{9,10},{10,11},{12,13},{... | collective-permute-start | bytes 3145736 | tf_op jit(solution)/shard_map/ppermute | solution.py:219
  159.3 36.6 %collective-permute-start.8 = (bf16[512,1024]{1,0:T(8,128)(2,1)}, bf16[512,1024]{1,0:T(8,128)(2,1)}, u32[]{:S(2)}, u32[]{:S(2)}) collective-permute-start(bf16[512,1024]{1,0:T(8,128)(2,1)} %add_convert_fusion.1), channel_id=1, source_target_pairs={{1,0},{2,1},{3,2},{5,4},{6,5},{7,6},{9,8},{10,9},{11,10},{13,12},{... | collective-permute-start | bytes 3145736 | tf_op jit(solution)/shard_map/ppermute | solution.py:222
  168.8 20.7 %collective-permute-start.17 = (bf16[1,8,128,128]{3,2,1,0:T(8,128)(2,1)S(1)}, bf16[1,8,128,128]{3,2,1,0:T(8,128)(2,1)S(1)}, u32[]{:S(2)}, u32[]{:S(2)}) collective-permute-start(bf16[1,8,128,128]{3,2,1,0:T(8,128)(2,1)S(1)} %fusion.19), channel_id=1, source_target_pairs={{0,16},{4,20},{8,24},{12,28},{16,0},{20,4},{24,8},{28,12},{1,17},{... | collective-permute-start | bytes 786440 | tf_op jit(solution)/shard_map/ppermute | solution.py:118
  170.3 1.2 copy-start.6
  171.5 1.1 copy-start.8

commit v2 on v0

v2 whole, which is shorter than its diff:
```python
import functools

import jax
import jax.numpy as jnp
from jax import lax
from jax.experimental import pallas as pl
from jax.experimental.pallas import tpu as pltpu
from jax.sharding import PartitionSpec as P

SPAN = 64
F32 = jnp.float32
BF16 = jnp.bfloat16
MESH = pl.DeviceIdType.MESH


def mm(a, b, ca=1, cb=0):
    return lax.dot_general(a, b, (((ca,), (cb,)), ((), ())), preferred_element_type=F32)


def table(seg_col, seg_row, rows, near):
    t = lax.broadcasted_iota(jnp.int32, (rows, rows), 0)
    s = lax.broadcasted_iota(jnp.int32, (rows, rows), 1)
    differ = jnp.bitwise_xor(t // SPAN, s // SPAN)
    level = jnp.zeros((rows, rows), jnp.int32)
    for section in range(near - 1):
        level = level + (differ >= 1 << section).astype(jnp.int32)
    return jnp.where((t >= s) & (seg_col == seg_row), level, near)


def kernel(
    n_ctx,
    n_head,
    heads,
    levels,
    near,
    q_ref,
    k_ref,
    v_ref,
    og_ref,
    ext_ref,
    w_hbm,
    mixed_ref,
    dq_ref,
    dk_ref,
    dv_ref,
    w_ref,
    gath,
    acc,
    near_out,
    pj,
    rsr,
    rsl,
    weights,
    probs,
    table_ref,
    cols_ref,
    cot,
    state_out,
    state_in,
    marks_out,
    marks_in,
    pieces,
    dual_out,
    dual_in,
    inbound,
    w_sem,
    ag_recv,
    ag_right,
    ag_left,
    rs_recv_r,
    rs_recv_l,
    rs_right,
    rs_left,
    st_send,
    st_recv,
    mk_send,
    mk_recv,
    du_send,
    du_recv,
):
    rows = q_ref.shape[0]
    dk = q_ref.shape[1] // heads
    dv = v_ref.shape[1] // heads
    width = og_ref.shape[1]
    inner = w_ref.shape[0]
    far = levels - near
    spread = n_ctx.bit_length() - 1
    me = lax.axis_index("ctx")
    z = lax.axis_index("head")
    not_first = z > 0
    not_last = z < n_head - 1
    bits = [(me // (1 << s)) % 2 for s in range(spread)]
    partners = [me + (1 - 2 * bits[s]) * (1 << s) for s in range(spread)]

    def remote(src, dst, send, recv, device):
        return pltpu.make_async_remote_copy(
            src_ref=src,
            dst_ref=dst,
            send_sem=send,
            recv_sem=recv,
            device_id=device,
            device_id_type=MESH,
        )

    load = pltpu.make_async_copy(w_hbm, w_ref, w_sem)
    load.start()

    barrier = pltpu.get_barrier_semaphore()
    for s in range(spread):
        pl.semaphore_signal(barrier, inc=1, device_id=(partners[s], z), device_id_type=MESH)

    @pl.when(not_first)
    def _():
        pl.semaphore_signal(barrier, inc=1, device_id=(me, z - 1), device_id_type=MESH)

    @pl.when(not_last)
    def _():
        pl.semaphore_signal(barrier, inc=1, device_id=(me, z + 1), device_id_type=MESH)

    pl.semaphore_wait(
        barrier, spread + not_first.astype(jnp.int32) + not_last.astype(jnp.int32)
    )

    def own_right():
        return remote(og_ref, gath.at[z], ag_right.at[z], ag_recv.at[z], (me, z + 1))

    def own_left():
        return remote(og_ref, gath.at[z], ag_left.at[z], ag_recv.at[z], (me, z - 1))

    def pass_right(owner):
        return remote(
            gath.at[owner], gath.at[owner], ag_right.at[owner], ag_recv.at[owner], (me, z + 1)
        )

    def pass_left(owner):
        return remote(
            gath.at[owner], gath.at[owner], ag_left.at[owner], ag_recv.at[owner], (me, z - 1)
        )

    @pl.when(not_last)
    def _():
        own_right().start()

    @pl.when(not_first)
    def _():
        own_left().start()

    def head_k(h):
        return pl.ds(pl.multiple_of(h * dk, dk), dk)

    def head_v(h):
        return pl.ds(pl.multiple_of(h * dv, dv), dv)

    @pl.loop(0, heads)
    def _(h):
        cols = ext_ref[h].T
        cols_ref[h] = cols
        seg = cols[:, levels : levels + 1]
        keep = (seg == seg[rows - 1 : rows, :]).astype(F32)
        masked = (k_ref[:, head_k(h)].astype(F32) * keep).astype(BF16)
        state_out[0, h] = mm(masked, v_ref[:, head_v(h)], 0, 0).astype(BF16)

    seg_row = ext_ref[0, levels : levels + 1, :]
    lane = dv
    first = jnp.broadcast_to(seg_row[:, 0:1], (1, lane))
    last = jnp.broadcast_to(seg_row[:, rows - 1 : rows], (1, lane))
    marks_out[0, 0:8, :] = jnp.broadcast_to(first, (8, lane))
    marks_out[0, 8:16, :] = jnp.broadcast_to(last, (8, lane))

    def hop(s):
        return (
            remote(
                state_out.at[s], state_in.at[s], st_send.at[s], st_recv.at[s], (partners[s], z)
            ),
            remote(
                marks_out.at[s], marks_in.at[s], mk_send.at[s], mk_recv.at[s], (partners[s], z)
            ),
        )

    def hop_start(s):
        for copy in hop(s):
            copy.start()

    def hop_finish(s):
        for copy in hop(s):
            copy.wait_recv()
        up = bits[s].astype(F32)
        own_first, own_last = marks_out[s, 0:1, :], marks_out[s, 8:9, :]
        its_first, its_last = marks_in[s, 0:1, :], marks_in[s, 8:9, :]
        joined = (its_last == own_last).astype(F32)
        linked = (its_last == first).astype(F32) * up
        mine = up + (1 - up) * joined
        theirs = (1 - up) + up * joined
        last_section = s == spread - 1

        @pl.loop(0, heads)
        def _(h):
            partner = state_in[s, h].astype(F32)
            pieces[s, h] = (partner * linked).astype(BF16)
            if not last_section:
                state_out[s + 1, h] = (
                    state_out[s, h].astype(F32) * mine + partner * theirs
                ).astype(BF16)

        if not last_section:
            marks_out[s + 1, 0:8, :] = jnp.broadcast_to(
                up * its_first + (1 - up) * own_first, (8, lane)
            )
            marks_out[s + 1, 8:16, :] = jnp.broadcast_to(
                up * own_last + (1 - up) * its_last, (8, lane)
            )
            hop_start(s + 1)

    if spread:
        hop_start(0)

    table_ref[...] = table(
        cols_ref[0][:, levels : levels + 1], ext_ref[0, levels : levels + 1, :], rows, near
    )
    tile = 256

    def near_forward(low, high):
        @pl.loop(low, high)
        def _(h):
            cols = cols_ref[h]
            level = table_ref[...]
            weight = jnp.zeros((rows, rows), F32)
            for j in range(near):
                weight = jnp.where(level == j, cols[:, j : j + 1], weight)
            weights[h] = weight.astype(BF16)
            p = (weight * mm(q_ref[:, head_k(h)], k_ref[:, head_k(h)], 1, 1)).astype(BF16)
            probs[h] = p
            near_out[:, head_v(h)] = mm(p, v_ref[:, head_v(h)])

    done = 0
    for s in range(spread):
        upto = heads * (s + 1) // spread
        near_forward(done, upto)
        done = upto
        hop_finish(s)
    if done < heads:
        near_forward(done, heads)

    def far_gates(h):
        cols = cols_ref[h]
        seg = cols[:, levels : levels + 1]
        keep = (seg == seg[0:1, :]).astype(F32)
        return [cols[:, near + j : near + j + 1] * keep for j in range(far)]

    @pl.loop(0, heads)
    def _(h):
        gates = far_gates(h)
        q = q_ref[:, head_k(h)]
        out = near_out[:, head_v(h)]
        for j in range(far):
            out = out + gates[j] * mm(q, pieces[j, h])
        mixed_ref[:, head_v(h)] = out.astype(BF16)

    load.wait()

    flip = (z < n_head - z).astype(jnp.int32)
    for at in range(n_head):
        dest = flip * (n_head - 1 - at) + (1 - flip) * at

        @pl.loop(0, width // tile)
        def _(c):
            from_col = pl.multiple_of(dest * width + c * tile, tile)
            part = mm(mixed_ref[...], w_ref[:, pl.ds(from_col, tile)])
            pj[dest, :, pl.ds(pl.multiple_of(c * tile, tile), tile)] = part.astype(BF16)

    def product(block, owner, fresh):
        @pl.loop(0, inner // tile)
        def _(r):
            at = pl.ds(pl.multiple_of(r * tile, tile), tile)
            part = mm(
                block[...], w_ref[at, pl.ds(pl.multiple_of(owner * width, width), width)], 1, 1
            )
            acc[:, at] = part if fresh else acc[:, at] + part

    product(og_ref, z, True)

    def sum_right(dest, src=rsr):
        return remote(src.at[dest], rsr.at[dest], rs_right.at[dest], rs_recv_r.at[dest], (me, z + 1))

    def sum_left(dest, src=rsl):
        return remote(src.at[dest], rsl.at[dest], rs_left.at[dest], rs_recv_l.at[dest], (me, z - 1))

    def add_rows(buf, dest):
        @pl.loop(0, rows // 64)
        def _(r):
            at = pl.ds(pl.multiple_of(r * 64, 64), 64)
            buf[dest, at, :] = (buf[dest, at, :].astype(F32) + pj[dest, at, :].astype(F32)).astype(
                BF16
            )

    def send_sum(buf, make, has_upstream, dest):
        @pl.when(has_upstream)
        def _():
            make(dest).wait_recv()
            add_rows(buf, dest)
            make(dest).start()

        @pl.when(jnp.logical_not(has_upstream))
        def _():
            make(dest, pj).start()

    for phase in range(1, n_head):
        reach = n_head - phase
        from_left, from_right = z - phase, z + phase
        has_left, has_right = from_left >= 0, from_right < n_head

        @pl.when(has_left)
        def _():
            pass_right(from_left).wait_recv()

            @pl.when(not_last)
            def _():
                pass_right(from_left).start()

        @pl.when(has_right)
        def _():
            pass_left(from_right).wait_recv()

            @pl.when(not_first)
            def _():
                pass_left(from_right).start()

        @pl.when(z + reach < n_head)
        def _():
            send_sum(rsr, sum_right, not_first, z + reach)

        @pl.when(z - reach >= 0)
        def _():
            send_sum(rsl, sum_left, not_last, z - reach)

        @pl.when(has_left)
        def _():
            product(gath.at[from_left], from_left, False)

        @pl.when(has_right)
        def _():
            product(gath.at[from_right], from_right, False)

    @pl.loop(0, heads)
    def _(h):
        g = acc[:, head_v(h)].astype(BF16)
        cot[:, head_v(h)] = g
        g = g.astype(F32)
        q = q_ref[:, head_k(h)]
        gates = far_gates(h)
        for j in range(far):
            dual_out[j, h] = mm(q, (g * gates[j]).astype(BF16), 0, 0).astype(BF16)

    starts = [sum(spread - i for i in range(s)) for s in range(spread + 1)]

    def dual_hop(s):
        block = pl.ds(starts[s], spread - s)
        return remote(
            dual_out.at[block], dual_in.at[block], du_send.at[s], du_recv.at[s], (partners[s], z)
        )

    def dual_finish(s):
        dual_hop(s).wait_recv()
        up = bits[s].astype(F32)
        own_first, its_first = marks_out[s, 0:1, :], marks_in[s, 0:1, :]
        joined = (its_first == own_first).astype(F32)
        linked = (its_first == last).astype(F32) * (1 - up)
        mine = (1 - up) + up * joined
        theirs = up + (1 - up) * joined

        @pl.loop(0, heads)
        def _(h):
            gain = dual_in[starts[s], h].astype(F32) * linked
            inbound[h] = gain if s == 0 else inbound[h] + gain
            for j in range(1, spread - s):
                dual_out[starts[s + 1] + j - 1, h] = (
                    dual_out[starts[s] + j, h].astype(F32) * mine
                    + dual_in[starts[s] + j, h].astype(F32) * theirs
                ).astype(BF16)

        if s < spread - 1:
            dual_hop(s + 1).start()

    if spread:
        dual_hop(0).start()

    def near_backward(low, high):
        @pl.loop(low, high)
        def _(h):
            q, k = q_ref[:, head_k(h)], k_ref[:, head_k(h)]
            v, g = v_ref[:, head_v(h)], cot[:, head_v(h)]
            near_out[:, head_v(h)] = mm(probs[h], g, 0, 0)
            grads = (weights[h].astype(F32) * mm(g, v, 1, 1)).astype(BF16)
            acc[:, head_k(h)] = mm(grads, q, 0, 0)
            dq = mm(grads, k)
            gates = far_gates(h)
            for j in range(far):
                dq = dq + gates[j] * mm(g, pieces[j, h], 1, 1)
            dq_ref[:, head_k(h)] = dq.astype(BF16)

    done = 0
    for s in range(spread):
        upto = heads * (s + 1) // spread
        near_backward(done, upto)
        done = upto
        dual_finish(s)
    if done < heads:
        near_backward(done, heads)

    @pl.loop(0, heads)
    def _(h):
        seg = cols_ref[h][:, levels : levels + 1]
        keep = (seg == seg[rows - 1 : rows, :]).astype(F32)
        near_dk, near_dv = acc[:, head_k(h)], near_out[:, head_v(h)]
        if spread:
            state = inbound[h].astype(BF16)
            near_dk = near_dk + keep * mm(v_ref[:, head_v(h)], state, 1, 1)
            near_dv = near_dv + keep * mm(k_ref[:, head_k(h)], state)
        dk_ref[:, head_k(h)] = near_dk.astype(BF16)
        dv_ref[:, head_v(h)] = near_dv.astype(BF16)

    acc[...] = pj[z].astype(F32)

    @pl.when(not_first)
    def _():
        sum_right(z).wait_recv()
        acc[...] = acc[...] + rsr[z].astype(F32)

    @pl.when(not_last)
    def _():
        sum_left(z).wait_recv()
        acc[...] = acc[...] + rsl[z].astype(F32)

    mixed_ref[...] = acc[...].astype(BF16)

    @pl.when(not_last)
    def _():
        own_right().wait_send()

    @pl.when(not_first)
    def _():
        own_left().wait_send()

    for phase in range(1, n_head):
        reach = n_head - phase

        @pl.when((z - phase >= 0) & not_last)
        def _():
            pass_right(z - phase).wait_send()

        @pl.when((z + phase < n_head) & not_first)
        def _():
            pass_left(z + phase).wait_send()

        @pl.when(z + reach < n_head)
        def _():
            sum_right(z + reach).wait_send()

        @pl.when(z - reach >= 0)
        def _():
            sum_left(z - reach).wait_send()

    for s in range(spread):
        for copy in hop(s):
            copy.wait_send()
        dual_hop(s).wait_send()


def shards(queries, keys, values, gates, segment_ids, out_weight, out_grad):
    rows = queries.shape[0]
    heads, levels = gates.shape[0], gates.shape[1]
    dk = queries.shape[1] // heads
    dv = values.shape[1] // heads
    near = (rows // SPAN).bit_length()
    n_ctx = lax.axis_size("ctx")
    n_head = lax.axis_size("head")
    spread = n_ctx.bit_length() - 1
    width = out_grad.shape[1]
    inner = out_weight.shape[0]
    size = -(-(levels + 1) // 8) * 8
    ext = jnp.concatenate(
        [
            gates,
            jnp.broadcast_to(segment_ids.astype(F32), (heads, 1, rows)),
            jnp.zeros((heads, size - levels - 1, rows), F32),
        ],
        axis=1,
    )
    duals = max(spread * (spread + 1) // 2, 1)
    hops = max(spread, 1)
    dma = pltpu.SemaphoreType.DMA
    vmem = pl.BlockSpec(memory_space=pltpu.VMEM)
    return pl.pallas_call(
        functools.partial(kernel, n_ctx, n_head, heads, levels, near),
        in_specs=[vmem] * 5 + [pl.BlockSpec(memory_space=pl.ANY)],
        out_specs=[vmem] * 4,
        out_shape=[
            jax.ShapeDtypeStruct((rows, width), BF16),
            jax.ShapeDtypeStruct(queries.shape, BF16),
            jax.ShapeDtypeStruct(keys.shape, BF16),
            jax.ShapeDtypeStruct(values.shape, BF16),
        ],
        scratch_shapes=[
            pltpu.VMEM(out_weight.shape, BF16),
            pltpu.VMEM((n_head, rows, width), BF16),
            pltpu.VMEM((rows, inner), F32),
            pltpu.VMEM((rows, inner), F32),
            pltpu.VMEM((n_head, rows, width), BF16),
            pltpu.VMEM((n_head, rows, width), BF16),
            pltpu.VMEM((n_head, rows, width), BF16),
            pltpu.VMEM((heads, rows, rows), BF16),
            pltpu.VMEM((heads, rows, rows), BF16),
            pltpu.VMEM((rows, rows), jnp.int32),
            pltpu.VMEM((heads, rows, size), F32),
            pltpu.VMEM((rows, inner), BF16),
            pltpu.VMEM((hops, heads, dk, dv), BF16),
            pltpu.VMEM((hops, heads, dk, dv), BF16),
            pltpu.VMEM((hops, 16, dv), F32),
            pltpu.VMEM((hops, 16, dv), F32),
            pltpu.VMEM((hops, heads, dk, dv), BF16),
            pltpu.VMEM((duals, heads, dk, dv), BF16),
            pltpu.VMEM((duals, heads, dk, dv), BF16),
            pltpu.VMEM((heads, dk, dv), F32),
            dma,
            dma((n_head,)),
            dma((n_head,)),
            dma((n_head,)),
            dma((n_head,)),
            dma((n_head,)),
            dma((n_head,)),
            dma((n_head,)),
            dma((hops,)),
            dma((hops,)),
            dma((hops,)),
            dma((hops,)),
            dma((hops,)),
            dma((hops,)),
        ],
        compiler_params=pltpu.CompilerParams(
            collective_id=0, has_side_effects=True, vmem_limit_bytes=60 << 20
        ),
        cost_estimate=pl.CostEstimate(
            flops=4 * rows * n_head * width * inner + 14 * rows * rows * dk * heads,
            bytes_accessed=40 << 20,
            transcendentals=0,
        ),
    )(queries, keys, values, out_grad, ext, out_weight)


def solution(mesh):
    placed = (
        P("ctx", "head"),
        P("ctx", "head"),
        P("ctx", "head"),
        P("head", None, "ctx"),
        P("ctx"),
        P("head", None),
        P("ctx", "head"),
    )

    def body(*args):
        return tuple(shards(*args))

    return jax.shard_map(
        body,
        mesh=mesh,
        in_specs=placed,
        out_specs=(P("ctx", "head"), P("ctx", "head"), P("ctx", "head"), P("ctx", "head")),
        check_vma=False,
    )
```

time: 179 us -> 132 us (0.74)
  Pallas kernels: 0 us -> 119 us
  waiting for transfers between devices: 52.9 us -> 0 us
  matrix products: 50.5 us -> 0 us
  between operations: 22.4 us -> 0.64 us
  starting transfers between devices: 17 us -> 0 us
  other arithmetic: 14.7 us -> 1.37 us
  local copies, waits for them, and re-layouts: 20.6 us -> 10 us
    pallas_call x0 -> x1, Pallas kernels: none -> 119 us  [shards(): pl.pallas_call(functools.partial(kernel, n_ctx, n_head, heads, levels, ne...]
    dot_general x19 -> x0, matrix products: 50.5 us -> none  [the longest x1 9.17 us: shards(): jnp.einsum('tc,rc->tr', lax.all_gather(out_grad, 'head', axis=1, tiled=Tr...]
    all_gather x1 -> x0, waiting for transfers between devices: 20.5 us -> none  [shards(): lax.all_gather(out_grad, 'head', axis=1, tiled=True)]
    ppermute x12 -> x0, waiting for transfers between devices: 18.5 us -> none  [from_partner(): return lax.ppermute(value, axis, pairs)]
    ppermute x12 -> x0, starting transfers between devices: 16.9 us -> none  [from_partner(): return lax.ppermute(value, axis, pairs)]
    reduce_scatter x1 -> x0, waiting for transfers between devices: 13.2 us -> none  [shards(): lax.psum_scatter(partial_value.astype(jnp.bfloat16), 'head', scatter_dime...]
    convert_element_type x6 -> x1, other arithmetic: 6.2 us -> 0.68 us  [shards(): segment_ids.astype(F32)]
    reshape x3 -> x0, local copies, waits for them, and re-layouts: 3.59 us -> none  [the longest x1 1.46 us: shards(): query_heads = queries.reshape(row_count, heads_here, key_width)]
  transfers between devices with their start and end apart: 14 -> 0, of which waited for: 9 -> 0; matrix products, arithmetic and copies ran while one was open for 46% -> 0% of each run, Pallas kernels for 0% -> 0%
where the time goes in v2:
time: 132 us; the launch traced here: 131 us
  Pallas kernels  119 us (90%)
  local copies, waits for them, and re-layouts  10 us (8%)
  other arithmetic  1.37 us (1%)
    pallas_call x1, Pallas kernels, shards(): pl.pallas_call(functools.partial(kernel, n_ctx, n_head, heads, levels, ne...  119 us
    unnamed x5, local copies, waits for them, and re-layouts  10 us

profile of v2, /device:TPU:0, one launch (start us, length us, event | category | flops | bytes accessed | tf_op | source)
XLA Modules:
  0.0 131.4 jit_solution(4033468182197181556)
XLA Ops:
  0.6 0.7 convert_element_type.3
  1.3 1.0 copy.11
  2.3 0.7 pad_maximum_fusion.ext_ref
  3.0 119.4 %shard_map.102 = (bf16[512,1024]{1,0:T(8,128)(2,1)}, bf16[512,1024]{1,0:T(8,128)(2,1)}, bf16[512,1024]{1,0:T(8,128)(2,1)}, bf16[512,1024]{1,0:T(8,128)(2,1)}) custom-call(bf16[512,1024]{1,0:T(8,128)(2,1)} %q_ref.1, bf16[512,1024]{1,0:T(8,128)(2,1)} %k_ref.1, bf16[512,1024]{1,0:T(8,128)(2,1)} %v_ref.1, bf16[512,1024]{1,0:T(8,128)(2,1)} %og_ref.1, ...), custom_call_target="tpu_custom_call" | custom-call | flops 12348030976 | bytes 41943040 | tf_op jit(solution)/shard_map/pallas_call | solution.py:493
  122.3 2.3 %copy.16 = bf16[512,1024]{1,0:T(8,128)(2,1)} copy(bf16[512,1024]{1,0:T(8,128)(2,1)} %get-tuple-element.8) | data formatting | bytes 2097152
  124.6 2.3 %copy.17 = bf16[512,1024]{1,0:T(8,128)(2,1)} copy(bf16[512,1024]{1,0:T(8,128)(2,1)} %get-tuple-element.9) | data formatting | bytes 2097152
  126.9 2.3 %copy.18 = bf16[512,1024]{1,0:T(8,128)(2,1)} copy(bf16[512,1024]{1,0:T(8,128)(2,1)} %get-tuple-element.10) | data formatting | bytes 2097152
  129.1 2.3 %copy.19 = bf16[512,1024]{1,0:T(8,128)(2,1)} copy(bf16[512,1024]{1,0:T(8,128)(2,1)} %get-tuple-element.11) | data formatting | bytes 2097152
  (1 shorter events, 0.0 us)

commit v3 on v2

--- a/solution.py
+++ b/solution.py
@@ -8,6 +8,7 @@
 from jax.sharding import PartitionSpec as P
 
 SPAN = 64
+PARTS = 2
 F32 = jnp.float32
 BF16 = jnp.bfloat16
 MESH = pl.DeviceIdType.MESH
@@ -77,6 +78,8 @@
     mk_recv,
     du_send,
     du_recv,
+    ds_send,
+    ds_recv,
 ):
     rows = q_ref.shape[0]
     dk = q_ref.shape[1] // heads
@@ -121,29 +124,48 @@
         barrier, spread + not_first.astype(jnp.int32) + not_last.astype(jnp.int32)
     )
 
-    def own_right():
-        return remote(og_ref, gath.at[z], ag_right.at[z], ag_recv.at[z], (me, z + 1))
-
-    def own_left():
-        return remote(og_ref, gath.at[z], ag_left.at[z], ag_recv.at[z], (me, z - 1))
-
-    def pass_right(owner):
+    slab = rows // PARTS
+
+    def part_rows(part):
+        return pl.ds(part * slab, slab)
+
+    def own_right(part):
         return remote(
-            gath.at[owner], gath.at[owner], ag_right.at[owner], ag_recv.at[owner], (me, z + 1)
-        )
-
-    def pass_left(owner):
+            og_ref.at[part_rows(part)],
+            gath.at[z, part_rows(part)],
+            ag_right.at[z, part],
+            ag_recv.at[z, part],
+            (me, z + 1),
+        )
+
+    def own_left(part):
         return remote(
-            gath.at[owner], gath.at[owner], ag_left.at[owner], ag_recv.at[owner], (me, z - 1)
-        )
-
-    @pl.when(not_last)
-    def _():
-        own_right().start()
-
-    @pl.when(not_first)
-    def _():
-        own_left().start()
+            og_ref.at[part_rows(part)],
+            gath.at[z, part_rows(part)],
+            ag_left.at[z, part],
+            ag_recv.at[z, part],
+            (me, z - 1),
+        )
+
+    def pass_right(owner, part):
+        block = gath.at[owner, part_rows(part)]
+        return remote(
+            block, block, ag_right.at[owner, part], ag_recv.at[owner, part], (me, z + 1)
+        )
+
+    def pass_left(owner, part):
+        block = gath.at[owner, part_rows(part)]
+        return remote(block, block, ag_left.at[owner, part], ag_recv.at[owner, part], (me, z - 1))
+
+    for part in range(PARTS):
+
+        @pl.when(not_last)
+        def _():
+            own_right(part).start()
+
+        @pl.when(not_first)
+        def _():
+            own_left(part).start()
 
     def head_k(h):
         return pl.ds(pl.multiple_of(h * dk, dk), dk)
@@ -259,7 +281,8 @@
     load.wait()
 
     flip = (z < n_head - z).astype(jnp.int32)
-    for at in range(n_head):
+
+    def project(at):
         dest = flip * (n_head - 1 - at) + (1 - flip) * at
 
         @pl.loop(0, width // tile)
@@ -268,78 +291,109 @@
             part = mm(mixed_ref[...], w_ref[:, pl.ds(from_col, tile)])
             pj[dest, :, pl.ds(pl.multiple_of(c * tile, tile), tile)] = part.astype(BF16)
 
-    def product(block, owner, fresh):
+    def product(block, owner, at_rows, fresh):
         @pl.loop(0, inner // tile)
         def _(r):
             at = pl.ds(pl.multiple_of(r * tile, tile), tile)
-            part = mm(
-                block[...], w_ref[at, pl.ds(pl.multiple_of(owner * width, width), width)], 1, 1
+            term = mm(
+                block[at_rows, :],
+                w_ref[at, pl.ds(pl.multiple_of(owner * width, width), width)],
+                1,
+                1,
             )
-            acc[:, at] = part if fresh else acc[:, at] + part
-
-    product(og_ref, z, True)
-
-    def sum_right(dest, src=rsr):
-        return remote(src.at[dest], rsr.at[dest], rs_right.at[dest], rs_recv_r.at[dest], (me, z + 1))
-
-    def sum_left(dest, src=rsl):
-        return remote(src.at[dest], rsl.at[dest], rs_left.at[dest], rs_recv_l.at[dest], (me, z - 1))
-
-    def add_rows(buf, dest):
-        @pl.loop(0, rows // 64)
-        def _(r):
-            at = pl.ds(pl.multiple_of(r * 64, 64), 64)
-            buf[dest, at, :] = (buf[dest, at, :].astype(F32) + pj[dest, at, :].astype(F32)).astype(
-                BF16
-            )
-
-    def send_sum(buf, make, has_upstream, dest):
+            acc[at_rows, at] = term if fresh else acc[at_rows, at] + term
+
+    def sum_right(dest, part, src=rsr):
+        return remote(
+            src.at[dest, part_rows(part)],
+            rsr.at[dest, part_rows(part)],
+            rs_right.at[dest, part],
+            rs_recv_r.at[dest, part],
+            (me, z + 1),
+        )
+
+    def sum_left(dest, part, src=rsl):
+        return remote(
+            src.at[dest, part_rows(part)],
+            rsl.at[dest, part_rows(part)],
+            rs_left.at[dest, part],
+            rs_recv_l.at[dest, part],
+            (me, z - 1),
+        )
+
+    def send_sum(buf, make, has_upstream, dest, part):
         @pl.when(has_upstream)
         def _():
-            make(dest).wait_recv()
-            add_rows(buf, dest)
-            make(dest).start()
+            make(dest, part).wait_recv()
+
+            @pl.loop(0, slab // 64)
+            def _(r):
+                at = pl.ds(pl.multiple_of(part * slab + r * 64, 64), 64)
+                buf[dest, at, :] = (
+                    buf[dest, at, :].astype(F32) + pj[dest, at, :].astype(F32)
+                ).astype(BF16)
+
+            make(dest, part).start()
 
         @pl.when(jnp.logical_not(has_upstream))
         def _():
-            make(dest, pj).start()
-
-    for phase in range(1, n_head):
+            make(dest, part, pj).start()
+
+    def sums(phase, part):
         reach = n_head - phase
-        from_left, from_right = z - phase, z + phase
-        has_left, has_right = from_left >= 0, from_right < n_head
-
-        @pl.when(has_left)
-        def _():
-            pass_right(from_left).wait_recv()
+
+        @pl.when(z + reach < n_head)
+        def _():
+            send_sum(rsr, sum_right, not_first, z + reach, part)
+
+        @pl.when(z - reach >= 0)
+        def _():
+            send_sum(rsl, sum_left, not_last, z - reach, part)
+
+    def forwards(phase, part):
+        @pl.when(z - phase >= 0)
+        def _():
+            pass_right(z - phase, part).wait_recv()
 
             @pl.when(not_last)
             def _():
-                pass_right(from_left).start()
-
-        @pl.when(has_right)
-        def _():
-            pass_left(from_right).wait_recv()
+                pass_right(z - phase, part).start()
+
+        @pl.when(z + phase < n_head)
+        def _():
+            pass_left(z + phase, part).wait_recv()
 
             @pl.when(not_first)
             def _():
-                pass_left(from_right).start()
-
-        @pl.when(z + reach < n_head)
-        def _():
-            send_sum(rsr, sum_right, not_first, z + reach)
-
-        @pl.when(z - reach >= 0)
-        def _():
-            send_sum(rsl, sum_left, not_last, z - reach)
-
-        @pl.when(has_left)
-        def _():
-            product(gath.at[from_left], from_left, False)
-
-        @pl.when(has_right)
-        def _():
-            product(gath.at[from_right], from_right, False)
+                pass_left(z + phase, part).start()
+
+    def products(phase, at_rows):
+        @pl.when(z - phase >= 0)
+        def _():
+            product(gath.at[z - phase], z - phase, at_rows, False)
+
+        @pl.when(z + phase < n_head)
+        def _():
+            product(gath.at[z + phase], z + phase, at_rows, False)
+
+    whole_block = pl.ds(0, rows)
+    project(0)
+    if n_head > 1:
+        for part in range(PARTS):
+            sums(1, part)
+        project(1)
+        for part in range(PARTS):
+            forwards(1, part)
+    for at in range(2, n_head):
+        project(at)
+    product(og_ref, z, whole_block, True)
+    if n_head > 1:
+        products(1, whole_block)
+    for phase in range(2, n_head):
+        for part in range(PARTS):
+            forwards(phase, part)
+            sums(phase, part)
+            products(phase, part_rows(part))
 
     @pl.loop(0, heads)
     def _(h):
@@ -353,14 +407,27 @@
 
     starts = [sum(spread - i for i in range(s)) for s in range(spread + 1)]
 
+    split = heads // 2 if heads % 2 == 0 else 0
+
     def dual_hop(s):
         block = pl.ds(starts[s], spread - s)
+        if s and split:
+            block = (block, pl.ds(bits[0] * split, split))
         return remote(
             dual_out.at[block], dual_in.at[block], du_send.at[s], du_recv.at[s], (partners[s], z)
         )
 
+    def dual_share(s):
+        block = (pl.ds(starts[s], spread - s), pl.ds(bits[0] * split, split))
+        return remote(
+            dual_in.at[block], dual_in.at[block], ds_send.at[s], ds_recv.at[s], (partners[0], z)
+        )
+
     def dual_finish(s):
         dual_hop(s).wait_recv()
+        if s and split:
+            dual_share(s).start()
+            dual_share(s).wait_recv()
         up = bits[s].astype(F32)
         own_first, its_first = marks_out[s, 0:1, :], marks_in[s, 0:1, :]
         joined = (its_first == own_first).astype(F32)
@@ -423,47 +490,53 @@
 
     @pl.when(not_first)
     def _():
-        sum_right(z).wait_recv()
+        for part in range(PARTS):
+            sum_right(z, part).wait_recv()
         acc[...] = acc[...] + rsr[z].astype(F32)
 
     @pl.when(not_last)
     def _():
-        sum_left(z).wait_recv()
+        for part in range(PARTS):
+            sum_left(z, part).wait_recv()
         acc[...] = acc[...] + rsl[z].astype(F32)
 
     mixed_ref[...] = acc[...].astype(BF16)
 
-    @pl.when(not_last)
-    def _():
-        own_right().wait_send()
-
-    @pl.when(not_first)
-    def _():
-        own_left().wait_send()
-
-    for phase in range(1, n_head):
-        reach = n_head - phase
-
-        @pl.when((z - phase >= 0) & not_last)
-        def _():
-            pass_right(z - phase).wait_send()
-
-        @pl.when((z + phase < n_head) & not_first)
-        def _():
-            pass_left(z + phase).wait_send()
-
-        @pl.when(z + reach < n_head)
-        def _():
-            sum_right(z + reach).wait_send()
-
-        @pl.when(z - reach >= 0)
-        def _():
-            sum_left(z - reach).wait_send()
+    for part in range(PARTS):
+
+        @pl.when(not_last)
+        def _():
+            own_right(part).wait_send()
+
+        @pl.when(not_first)
+        def _():
+            own_left(part).wait_send()
+
+        for phase in range(1, n_head):
+            reach = n_head - phase
+
+            @pl.when((z - phase >= 0) & not_last)
+            def _():
+                pass_right(z - phase, part).wait_send()
+
+            @pl.when((z + phase < n_head) & not_first)
+            def _():
+                pass_left(z + phase, part).wait_send()
+
+            @pl.when(z + reach < n_head)
+            def _():
+                sum_right(z + reach, part).wait_send()
+
+            @pl.when(z - reach >= 0)
+            def _():
+                sum_left(z - reach, part).wait_send()
 
     for s in range(spread):
         for copy in hop(s):
             copy.wait_send()
         dual_hop(s).wait_send()
+        if s and split:
+            dual_share(s).wait_send()
 
 
 def shards(queries, keys, values, gates, segment_ids, out_weight, out_grad):
@@ -522,13 +595,15 @@
             pltpu.VMEM((duals, heads, dk, dv), BF16),
             pltpu.VMEM((heads, dk, dv), F32),
             dma,
-            dma((n_head,)),
-            dma((n_head,)),
-            dma((n_head,)),
-            dma((n_head,)),
-            dma((n_head,)),
-            dma((n_head,)),
-            dma((n_head,)),
+            dma((n_head, PARTS)),
+            dma((n_head, PARTS)),
+            dma((n_head, PARTS)),
+            dma((n_head, PARTS)),
+            dma((n_head, PARTS)),
+            dma((n_head, PARTS)),
+            dma((n_head, PARTS)),
+            dma((hops,)),
+            dma((hops,)),
             dma((hops,)),
             dma((hops,)),
             dma((hops,)),
@@ -547,6 +622,26 @@
     )(queries, keys, values, out_grad, ext, out_weight)
 
 
+def copy_kernel(*refs):
+    half = len(refs) // 2
+    for source, target in zip(refs[:half], refs[half:]):
+        target[...] = source[...]
+
+
+def results(arrays):
+    spec = [pl.BlockSpec((a.shape[0] // 4, a.shape[1]), lambda i: (i, 0)) for a in arrays]
+    return tuple(
+        pl.pallas_call(
+            copy_kernel,
+            grid=(4,),
+            in_specs=spec,
+            out_specs=spec,
+            out_shape=[jax.ShapeDtypeStruct(a.shape, a.dtype) for a in arrays],
+            compiler_params=pltpu.CompilerParams(vmem_limit_bytes=60 << 20),
+        )(*arrays)
+    )
+
+
 def solution(mesh):
     placed = (
         P("ctx", "head"),
@@ -559,7 +654,7 @@
     )
 
     def body(*args):
-        return tuple(shards(*args))
+        return results(shards(*args))
 
     return jax.shard_map(
         body,

time: 132 us -> 117 us (0.89)
  local copies, waits for them, and re-layouts: 10 us -> 0.98 us
  Pallas kernels: 119 us -> 114 us
    pallas_call x1, Pallas kernels: 119 us -> 109 us  [shards(): pl.pallas_call(functools.partial(kernel, n_ctx, n_head, heads, levels, ne...]
    unnamed x5 -> x1, local copies, waits for them, and re-layouts: 10 us -> 0.97 us
    pallas_call x0 -> x1, Pallas kernels: none -> 4.66 us  [results(): pl.pallas_call(copy_kernel, grid=(4,), in_specs=spec, out_specs=spec, out...]
where the time goes in v3:
time: 117 us
  Pallas kernels  114 us (97%)
  other arithmetic  1.37 us (1%)
    pallas_call x1, Pallas kernels, shards(): pl.pallas_call(functools.partial(kernel, n_ctx, n_head, heads, levels, ne...  109 us
    pallas_call x1, Pallas kernels, results(): pl.pallas_call(copy_kernel, grid=(4,), in_specs=spec, out_specs=spec, out...  4.66 us

profile of v3, /device:TPU:0, one launch (start us, length us, event | category | flops | bytes accessed | tf_op | source)
XLA Modules:
  0.0 116.9 jit_solution(10168965749281735231)
XLA Ops:
  0.6 0.7 convert_element_type.3
  1.3 1.0 copy.11
  2.3 0.7 pad_maximum_fusion.ext_ref
  3.0 109.2 %shard_map.102 = (bf16[512,1024]{1,0:T(8,128)(2,1)}, bf16[512,1024]{1,0:T(8,128)(2,1)}, bf16[512,1024]{1,0:T(8,128)(2,1)}, bf16[512,1024]{1,0:T(8,128)(2,1)}) custom-call(bf16[512,1024]{1,0:T(8,128)(2,1)} %q_ref.1, bf16[512,1024]{1,0:T(8,128)(2,1)} %k_ref.1, bf16[512,1024]{1,0:T(8,128)(2,1)} %v_ref.1, bf16[512,1024]{1,0:T(8,128)(2,1)} %og_ref.1, ...), custom_call_target="tpu_custom_call" | custom-call | flops 12348030976 | bytes 41943040 | tf_op jit(solution)/shard_map/pallas_call | solution.py:566
  112.2 4.7 %shard_map.103 = (bf16[512,1024]{1,0:T(8,128)(2,1)}, bf16[512,1024]{1,0:T(8,128)(2,1)}, bf16[512,1024]{1,0:T(8,128)(2,1)}, bf16[512,1024]{1,0:T(8,128)(2,1)}) custom-call(bf16[512,1024]{1,0:T(8,128)(2,1)} %get-tuple-element.8.refs_0_, bf16[512,1024]{1,0:T(8,128)(2,1)} %get-tuple-element.9.refs_1_, bf16[512,1024]{1,0:T(8,128)(2,1)} %get-tuple-element.10.refs_2_, ...), custom_call_target="tpu_custom_call" | custom-call | tf_op jit(solution)/shard_map/pallas_call | solution.py:634
  (1 shorter events, 0.0 us)

commit v4 on v3

--- a/solution.py
+++ b/solution.py
@@ -34,16 +34,27 @@
     heads,
     levels,
     near,
+    q_hbm,
+    k_hbm,
+    v_hbm,
+    og_hbm,
+    w_hbm,
+    gates_ref,
+    seg_ref,
+    mixed_hbm,
+    dq_hbm,
+    dk_hbm,
+    dv_hbm,
     q_ref,
     k_ref,
     v_ref,
     og_ref,
-    ext_ref,
-    w_hbm,
     mixed_ref,
     dq_ref,
     dk_ref,
     dv_ref,
+    ext_ref,
+    leaf_acc,
     w_ref,
     gath,
     acc,
@@ -64,7 +75,8 @@
     dual_out,
     dual_in,
     inbound,
-    w_sem,
+    in_sem,
+    out_sem,
     ag_recv,
     ag_right,
     ag_left,
@@ -105,9 +117,12 @@
             device_id_type=MESH,
         )
 
-    load = pltpu.make_async_copy(w_hbm, w_ref, w_sem)
-    load.start()
-
+    loads = [
+        pltpu.make_async_copy(source, target, in_sem.at[i])
+        for i, (source, target) in enumerate(
+            ((k_hbm, k_ref), (v_hbm, v_ref), (q_hbm, q_ref), (og_hbm, og_ref), (w_hbm, w_ref))
+        )
+    ]
     barrier = pltpu.get_barrier_semaphore()
     for s in range(spread):
         pl.semaphore_signal(barrier, inc=1, device_id=(partners[s], z), device_id_type=MESH)
@@ -120,6 +135,14 @@
     def _():
         pl.semaphore_signal(barrier, inc=1, device_id=(me, z + 1), device_id_type=MESH)
 
+    for load in loads:
+        load.start()
+
+    for j in range(levels):
+        ext_ref[:, j, :] = gates_ref[j]
+    for j in range(levels, ext_ref.shape[1]):
+        ext_ref[:, j, :] = jnp.broadcast_to(seg_ref[...].astype(F32), (heads, rows))
+
     pl.semaphore_wait(
         barrier, spread + not_first.astype(jnp.int32) + not_last.astype(jnp.int32)
     )
@@ -131,7 +154,7 @@
 
     def own_right(part):
         return remote(
-            og_ref.at[part_rows(part)],
+            og_hbm.at[part_rows(part)],
             gath.at[z, part_rows(part)],
             ag_right.at[z, part],
             ag_recv.at[z, part],
@@ -140,7 +163,7 @@
 
     def own_left(part):
         return remote(
-            og_ref.at[part_rows(part)],
+            og_hbm.at[part_rows(part)],
             gath.at[z, part_rows(part)],
             ag_left.at[z, part],
             ag_recv.at[z, part],
@@ -172,6 +195,9 @@
 
     def head_v(h):
         return pl.ds(pl.multiple_of(h * dv, dv), dv)
+
+    loads[0].wait()
+    loads[1].wait()
 
     @pl.loop(0, heads)
     def _(h):
@@ -240,6 +266,7 @@
         cols_ref[0][:, levels : levels + 1], ext_ref[0, levels : levels + 1, :], rows, near
     )
     tile = 256
+    loads[2].wait()
 
     def near_forward(low, high):
         @pl.loop(low, high)
@@ -278,7 +305,8 @@
             out = out + gates[j] * mm(q, pieces[j, h])
         mixed_ref[:, head_v(h)] = out.astype(BF16)
 
-    load.wait()
+    loads[3].wait()
+    loads[4].wait()
 
     flip = (z < n_head - z).astype(jnp.int32)
 
@@ -375,6 +403,25 @@
         @pl.when(z + phase < n_head)
         def _():
             product(gath.at[z + phase], z + phase, at_rows, False)
+
+    def leaves(part):
+        at = part_rows(part)
+
+        @pl.loop(0, heads)
+        def _(h):
+            g = acc[at, head_v(h)].astype(BF16)
+            cot[at, head_v(h)] = g
+            g = g.astype(F32)
+            q = q_ref[at, head_k(h)]
+            gates = far_gates(h)
+            for j in range(far):
+                term = mm(q, (g * gates[j][part * slab : (part + 1) * slab]).astype(BF16), 0, 0)
+                if part:
+                    term = leaf_acc[j, h] + term
+                if part < PARTS - 1:
+                    leaf_acc[j, h] = term
+                else:
+                    dual_out[j, h] = term.astype(BF16)
 
     whole_block = pl.ds(0, rows)
     project(0)
@@ -394,16 +441,11 @@
             forwards(phase, part)
             sums(phase, part)
             products(phase, part_rows(part))
-
-    @pl.loop(0, heads)
-    def _(h):
-        g = acc[:, head_v(h)].astype(BF16)
-        cot[:, head_v(h)] = g
-        g = g.astype(F32)
-        q = q_ref[:, head_k(h)]
-        gates = far_gates(h)
-        for j in range(far):
-            dual_out[j, h] = mm(q, (g * gates[j]).astype(BF16), 0, 0).astype(BF16)
+            if phase == n_head - 1:
+                leaves(part)
+    if n_head < 3:
+        for part in range(PARTS):
+            leaves(part)
 
     starts = [sum(spread - i for i in range(s)) for s in range(spread + 1)]
 
@@ -450,6 +492,11 @@
 
     if spread:
         dual_hop(0).start()
+
+    stores = [
+        pltpu.make_async_copy(source, target, out_sem.at[i])
+        for i, (source, target) in enumerate(((dq_ref, dq_hbm), (dk_ref, dk_hbm), (dv_ref, dv_hbm)))
+    ]
 
     def near_backward(low, high):
         @pl.loop(low, high)
@@ -473,6 +520,7 @@
         dual_finish(s)
     if done < heads:
         near_backward(done, heads)
+    stores[0].start()
 
     @pl.loop(0, heads)
     def _(h):
@@ -486,21 +534,48 @@
         dk_ref[:, head_k(h)] = near_dk.astype(BF16)
         dv_ref[:, head_v(h)] = near_dv.astype(BF16)
 
-    acc[...] = pj[z].astype(F32)
-
-    @pl.when(not_first)
-    def _():
-        for part in range(PARTS):
+    stores[1].start()
+    stores[2].start()
+
+    def last_sum(part, upstream):
+        @pl.loop(0, slab // 64)
+        def _(r):
+            at = pl.ds(pl.multiple_of(part * slab + r * 64, 64), 64)
+            total = pj[z, at, :].astype(F32)
+            for buf in upstream:
+                total = total + buf[z, at, :].astype(F32)
+            mixed_ref[at, :] = total.astype(BF16)
+
+    def mixed_store(part):
+        return pltpu.make_async_copy(
+            mixed_ref.at[part_rows(part)], mixed_hbm.at[part_rows(part)], out_sem.at[3 + part]
+        )
+
+    for part in range(PARTS):
+
+        @pl.when(not_first)
+        def _():
             sum_right(z, part).wait_recv()
-        acc[...] = acc[...] + rsr[z].astype(F32)
-
-    @pl.when(not_last)
-    def _():
-        for part in range(PARTS):
+
+        @pl.when(not_last)
+        def _():
             sum_left(z, part).wait_recv()
-        acc[...] = acc[...] + rsl[z].astype(F32)
-
-    mixed_ref[...] = acc[...].astype(BF16)
+
+        @pl.when(not_first & not_last)
+        def _():
+            last_sum(part, (rsr, rsl))
+
+        @pl.when(not_first & jnp.logical_not(not_last))
+        def _():
+            last_sum(part, (rsr,))
+
+        @pl.when(not_last & jnp.logical_not(not_first))
+        def _():
+            last_sum(part, (rsl,))
+
+        if n_head == 1:
+            last_sum(part, ())
+        mixed_store(part).start()
 
     for part in range(PARTS):
 
@@ -537,6 +612,10 @@
         dual_hop(s).wait_send()
         if s and split:
             dual_share(s).wait_send()
+    for store in stores:
+        store.wait()
+    for part in range(PARTS):
+        mixed_store(part).wait()
 
 
 def shards(queries, keys, values, gates, segment_ids, out_weight, out_grad):
@@ -551,22 +630,15 @@
     width = out_grad.shape[1]
     inner = out_weight.shape[0]
     size = -(-(levels + 1) // 8) * 8
-    ext = jnp.concatenate(
-        [
-            gates,
-            jnp.broadcast_to(segment_ids.astype(F32), (heads, 1, rows)),
-            jnp.zeros((heads, size - levels - 1, rows), F32),
-        ],
-        axis=1,
-    )
     duals = max(spread * (spread + 1) // 2, 1)
     hops = max(spread, 1)
     dma = pltpu.SemaphoreType.DMA
     vmem = pl.BlockSpec(memory_space=pltpu.VMEM)
+    hbm = pl.BlockSpec(memory_space=pl.ANY)
     return pl.pallas_call(
         functools.partial(kernel, n_ctx, n_head, heads, levels, near),
-        in_specs=[vmem] * 5 + [pl.BlockSpec(memory_space=pl.ANY)],
-        out_specs=[vmem] * 4,
+        in_specs=[hbm] * 5 + [vmem] * 2,
+        out_specs=[hbm] * 4,
         out_shape=[
             jax.ShapeDtypeStruct((rows, width), BF16),
             jax.ShapeDtypeStruct(queries.shape, BF16),
@@ -574,6 +646,16 @@
             jax.ShapeDtypeStruct(values.shape, BF16),
         ],
         scratch_shapes=[
+            pltpu.VMEM(queries.shape, BF16),
+            pltpu.VMEM(keys.shape, BF16),
+            pltpu.VMEM(values.shape, BF16),
+            pltpu.VMEM(out_grad.shape, BF16),
+            pltpu.VMEM((rows, max(width, inner)), BF16),
+            pltpu.VMEM(queries.shape, BF16),
+            pltpu.VMEM(keys.shape, BF16),
+            pltpu.VMEM(values.shape, BF16),
+            pltpu.VMEM((heads, size, rows), F32),
+            pltpu.VMEM((levels - near, heads, dk, dv), F32),
             pltpu.VMEM(out_weight.shape, BF16),
             pltpu.VMEM((n_head, rows, width), BF16),
             pltpu.VMEM((rows, inner), F32),
@@ -594,7 +676,8 @@
             pltpu.VMEM((duals, heads, dk, dv), BF16),
             pltpu.VMEM((duals, heads, dk, dv), BF16),
             pltpu.VMEM((heads, dk, dv), F32),
-            dma,
+            dma((5,)),
+            dma((3 + PARTS,)),
             dma((n_head, PARTS)),
             dma((n_head, PARTS)),
             dma((n_head, PARTS)),
@@ -619,24 +702,43 @@
             bytes_accessed=40 << 20,
             transcendentals=0,
         ),
-    )(queries, keys, values, out_grad, ext, out_weight)
+    )(
+        queries,
+        keys,
+        values,
+        out_grad,
+        out_weight,
+        gates.transpose(1, 0, 2),
+        segment_ids.reshape(1, rows),
+    )
 
 
 def copy_kernel(*refs):
+    sems, refs = refs[-1], refs[:-1]
     half = len(refs) // 2
-    for source, target in zip(refs[:half], refs[half:]):
-        target[...] = source[...]
+    copies = []
+    for i in range(half):
+        slab = refs[i].shape[0] // 4
+        for j in range(4):
+            at = pl.ds(j * slab, slab)
+            copies.append(
+                pltpu.make_async_copy(refs[i].at[at], refs[half + i].at[at], sems.at[4 * i + j])
+            )
+    for copy in copies:
+        copy.start()
+    for copy in copies:
+        copy.wait()
 
 
 def results(arrays):
-    spec = [pl.BlockSpec((a.shape[0] // 4, a.shape[1]), lambda i: (i, 0)) for a in arrays]
+    spec = [pl.BlockSpec(memory_space=pl.ANY)] * len(arrays)
     return tuple(
         pl.pallas_call(
             copy_kernel,
-            grid=(4,),
             in_specs=spec,
             out_specs=spec,
             out_shape=[jax.ShapeDtypeStruct(a.shape, a.dtype) for a in arrays],
+            scratch_shapes=[pltpu.SemaphoreType.DMA((4 * len(arrays),))],
             compiler_params=pltpu.CompilerParams(vmem_limit_bytes=60 << 20),
         )(*arrays)
     )

time: 117 us -> 236 us (2.02)
  Pallas kernels: 114 us -> 235 us
    pallas_call x1, Pallas kernels: 4.66 us -> 128 us  [results(): pl.pallas_call(copy_kernel, in_specs=spec, out_specs=spec, out_shape=[jax...]
    pallas_call x1, Pallas kernels: 109 us -> 106 us  [shards(): pl.pallas_call(functools.partial(kernel, n_ctx, n_head, heads, levels, ne...]
where the time goes in v4:
time: 236 us; the launch traced here: 235 us
  Pallas kernels  235 us (100%)
    pallas_call x1, Pallas kernels, results(): pl.pallas_call(copy_kernel, in_specs=spec, out_specs=spec, out_shape=[jax...  128 us
    pallas_call x1, Pallas kernels, shards(): pl.pallas_call(functools.partial(kernel, n_ctx, n_head, heads, levels, ne...  106 us

profile of v4, /device:TPU:0, one launch (start us, length us, event | category | flops | bytes accessed | tf_op | source)
XLA Modules:
  0.0 235.4 jit_solution(14841771185142301901)
XLA Ops:
  0.6 106.5 %shard_map.102 = (bf16[512,1024]{1,0:T(8,128)(2,1)}, bf16[512,1024]{1,0:T(8,128)(2,1)}, bf16[512,1024]{1,0:T(8,128)(2,1)}, bf16[512,1024]{1,0:T(8,128)(2,1)}) custom-call(bf16[512,1024]{1,0:T(8,128)(2,1)} %q_hbm.1, bf16[512,1024]{1,0:T(8,128)(2,1)} %k_hbm.1, bf16[512,1024]{1,0:T(8,128)(2,1)} %v_hbm.1, bf16[512,1024]{1,0:T(8,128)(2,1)} %og_hbm.1, ...), custom_call_target="tpu_custom_call" | custom-call | flops 12348030976 | bytes 41943040 | tf_op jit(solution)/shard_map/pallas_call | solution.py:638
  107.1 128.3 %shard_map.103 = (bf16[512,1024]{1,0:T(8,128)(2,1)}, bf16[512,1024]{1,0:T(8,128)(2,1)}, bf16[512,1024]{1,0:T(8,128)(2,1)}, bf16[512,1024]{1,0:T(8,128)(2,1)}) custom-call(bf16[512,1024]{1,0:T(8,128)(2,1)} %get-tuple-element.8.refs_0_, bf16[512,1024]{1,0:T(8,128)(2,1)} %get-tuple-element.9.refs_1_, bf16[512,1024]{1,0:T(8,128)(2,1)} %get-tuple-element.10.refs_2_, ...), custom_call_target="tpu_custom_call" | custom-call | tf_op jit(solution)/shard_map/pallas_call | solution.py:736

commit v5 on v4

--- a/solution.py
+++ b/solution.py
@@ -92,6 +92,8 @@
     du_recv,
     ds_send,
     ds_recv,
+    fs_send,
+    fs_recv,
 ):
     rows = q_ref.shape[0]
     dk = q_ref.shape[1] // heads
@@ -215,16 +217,30 @@
     marks_out[0, 0:8, :] = jnp.broadcast_to(first, (8, lane))
     marks_out[0, 8:16, :] = jnp.broadcast_to(last, (8, lane))
 
+    split = heads // 2 if heads % 2 == 0 else 0
+
+    def own_half():
+        return pl.ds(bits[0] * split, split)
+
     def hop(s):
+        block = (s, own_half()) if s and split else s
         return (
             remote(
-                state_out.at[s], state_in.at[s], st_send.at[s], st_recv.at[s], (partners[s], z)
+                state_out.at[block],
+                state_in.at[block],
+                st_send.at[s],
+                st_recv.at[s],
+                (partners[s], z),
             ),
             remote(
                 marks_out.at[s], marks_in.at[s], mk_send.at[s], mk_recv.at[s], (partners[s], z)
             ),
         )
 
+    def hop_share(s):
+        block = state_in.at[s, own_half()]
+        return remote(block, block, fs_send.at[s], fs_recv.at[s], (partners[0], z))
+
     def hop_start(s):
         for copy in hop(s):
             copy.start()
@@ -232,6 +248,9 @@
     def hop_finish(s):
         for copy in hop(s):
             copy.wait_recv()
+        if s and split:
+            hop_share(s).start()
+            hop_share(s).wait_recv()
         up = bits[s].astype(F32)
         own_first, own_last = marks_out[s, 0:1, :], marks_out[s, 8:9, :]
         its_first, its_last = marks_in[s, 0:1, :], marks_in[s, 8:9, :]
@@ -266,20 +285,25 @@
         cols_ref[0][:, levels : levels + 1], ext_ref[0, levels : levels + 1, :], rows, near
     )
     tile = 256
+    middle = rows // 2
     loads[2].wait()
 
     def near_forward(low, high):
         @pl.loop(low, high)
         def _(h):
             cols = cols_ref[h]
-            level = table_ref[...]
-            weight = jnp.zeros((rows, rows), F32)
-            for j in range(near):
-                weight = jnp.where(level == j, cols[:, j : j + 1], weight)
-            weights[h] = weight.astype(BF16)
-            p = (weight * mm(q_ref[:, head_k(h)], k_ref[:, head_k(h)], 1, 1)).astype(BF16)
-            probs[h] = p
-            near_out[:, head_v(h)] = mm(p, v_ref[:, head_v(h)])
+            weights[h, 0:middle, middle:rows] = jnp.zeros((middle, rows - middle), BF16)
+            probs[h, 0:middle, middle:rows] = jnp.zeros((middle, rows - middle), BF16)
+            for low_row, high_row in ((0, middle), (middle, rows)):
+                level = table_ref[low_row:high_row, 0:high_row]
+                weight = jnp.zeros(level.shape, F32)
+                for j in range(near):
+                    weight = jnp.where(level == j, cols[low_row:high_row, j : j + 1], weight)
+                weights[h, low_row:high_row, 0:high_row] = weight.astype(BF16)
+                scores = mm(q_ref[low_row:high_row, head_k(h)], k_ref[0:high_row, head_k(h)], 1, 1)
+                p = (weight * scores).astype(BF16)
+                probs[h, low_row:high_row, 0:high_row] = p
+                near_out[low_row:high_row, head_v(h)] = mm(p, v_ref[0:high_row, head_v(h)])
 
     done = 0
     for s in range(spread):
@@ -310,14 +334,14 @@
 
     flip = (z < n_head - z).astype(jnp.int32)
 
-    def project(at):
+    def project(at, at_rows):
         dest = flip * (n_head - 1 - at) + (1 - flip) * at
 
         @pl.loop(0, width // tile)
         def _(c):
             from_col = pl.multiple_of(dest * width + c * tile, tile)
-            part = mm(mixed_ref[...], w_ref[:, pl.ds(from_col, tile)])
-            pj[dest, :, pl.ds(pl.multiple_of(c * tile, tile), tile)] = part.astype(BF16)
+            part = mm(mixed_ref[at_rows, :], w_ref[:, pl.ds(from_col, tile)])
+            pj[dest, at_rows, pl.ds(pl.multiple_of(c * tile, tile), tile)] = part.astype(BF16)
 
     def product(block, owner, at_rows, fresh):
         @pl.loop(0, inner // tile)
@@ -424,15 +448,16 @@
                     dual_out[j, h] = term.astype(BF16)
 
     whole_block = pl.ds(0, rows)
-    project(0)
+    for part in range(PARTS):
+        project(0, part_rows(part))
+        if n_head > 1:
+            sums(1, part)
     if n_head > 1:
-        for part in range(PARTS):
-            sums(1, part)
-        project(1)
+        project(1, whole_block)
         for part in range(PARTS):
             forwards(1, part)
     for at in range(2, n_head):
-        project(at)
+        project(at, whole_block)
     product(og_ref, z, whole_block, True)
     if n_head > 1:
         products(1, whole_block)
@@ -449,8 +474,6 @@
 
     starts = [sum(spread - i for i in range(s)) for s in range(spread + 1)]
 
-    split = heads // 2 if heads % 2 == 0 else 0
-
     def dual_hop(s):
         block = pl.ds(starts[s], spread - s)
         if s and split:
@@ -612,6 +635,7 @@
         dual_hop(s).wait_send()
         if s and split:
             dual_share(s).wait_send()
+            hop_share(s).wait_send()
     for store in stores:
         store.wait()
     for part in range(PARTS):
@@ -693,6 +717,8 @@
             dma((hops,)),
             dma((hops,)),
             dma((hops,)),
+            dma((hops,)),
+            dma((hops,)),
         ],
         compiler_params=pltpu.CompilerParams(
             collective_id=0, has_side_effects=True, vmem_limit_bytes=60 << 20
@@ -714,20 +740,27 @@
 
 
 def copy_kernel(*refs):
-    sems, refs = refs[-1], refs[:-1]
-    half = len(refs) // 2
-    copies = []
-    for i in range(half):
-        slab = refs[i].shape[0] // 4
-        for j in range(4):
+    count = (len(refs) - 2) // 3
+    sources, targets, held = refs[:count], refs[count : 2 * count], refs[2 * count : 3 * count]
+    into, out = refs[-2], refs[-1]
+    pairs = []
+    for i in range(count):
+        slab = sources[i].shape[0] // 2
+        for j in range(2):
             at = pl.ds(j * slab, slab)
-            copies.append(
-                pltpu.make_async_copy(refs[i].at[at], refs[half + i].at[at], sems.at[4 * i + j])
+            pairs.append(
+                (
+                    pltpu.make_async_copy(sources[i].at[at], held[i].at[at], into.at[2 * i + j]),
+                    pltpu.make_async_copy(held[i].at[at], targets[i].at[at], out.at[2 * i + j]),
+                )
             )
-    for copy in copies:
-        copy.start()
-    for copy in copies:
-        copy.wait()
+    for first, _ in pairs:
+        first.start()
+    for first, second in pairs:
+        first.wait()
+        second.start()
+    for _, second in pairs:
+        second.wait()
 
 
 def results(arrays):
@@ -738,7 +771,8 @@
             in_specs=spec,
             out_specs=spec,
             out_shape=[jax.ShapeDtypeStruct(a.shape, a.dtype) for a in arrays],
-            scratch_shapes=[pltpu.SemaphoreType.DMA((4 * len(arrays),))],
+            scratch_shapes=[pltpu.VMEM(a.shape, a.dtype) for a in arrays]
+            + [pltpu.SemaphoreType.DMA((2 * len(arrays),))] * 2,
             compiler_params=pltpu.CompilerParams(vmem_limit_bytes=60 << 20),
         )(*arrays)
     )

time: 236 us -> 108 us (0.46)
  Pallas kernels: 235 us -> 108 us
    pallas_call x1, Pallas kernels: 128 us -> 3.58 us  [results(): pl.pallas_call(copy_kernel, in_specs=spec, out_specs=spec, out_shape=[jax...]
    pallas_call x1, Pallas kernels: 106 us -> 104 us  [shards(): pl.pallas_call(functools.partial(kernel, n_ctx, n_head, heads, levels, ne...]
where the time goes in v5:
time: 108 us
  Pallas kernels  108 us (100%)
    pallas_call x1, Pallas kernels, shards(): pl.pallas_call(functools.partial(kernel, n_ctx, n_head, heads, levels, ne...  104 us
    pallas_call x1, Pallas kernels, results(): pl.pallas_call(copy_kernel, in_specs=spec, out_specs=spec, out_shape=[jax...  3.58 us

profile of v5, /device:TPU:0, one launch (start us, length us, event | category | flops | bytes accessed | tf_op | source)
XLA Modules:
  0.0 108.3 jit_solution(5467113998056946341)
XLA Ops:
  0.6 104.1 %shard_map.102 = (bf16[512,1024]{1,0:T(8,128)(2,1)}, bf16[512,1024]{1,0:T(8,128)(2,1)}, bf16[512,1024]{1,0:T(8,128)(2,1)}, bf16[512,1024]{1,0:T(8,128)(2,1)}) custom-call(bf16[512,1024]{1,0:T(8,128)(2,1)} %q_hbm.1, bf16[512,1024]{1,0:T(8,128)(2,1)} %k_hbm.1, bf16[512,1024]{1,0:T(8,128)(2,1)} %v_hbm.1, bf16[512,1024]{1,0:T(8,128)(2,1)} %og_hbm.1, ...), custom_call_target="tpu_custom_call" | custom-call | flops 12348030976 | bytes 41943040 | tf_op jit(solution)/shard_map/pallas_call | solution.py:662
  104.7 3.6 %shard_map.103 = (bf16[512,1024]{1,0:T(8,128)(2,1)}, bf16[512,1024]{1,0:T(8,128)(2,1)}, bf16[512,1024]{1,0:T(8,128)(2,1)}, bf16[512,1024]{1,0:T(8,128)(2,1)}) custom-call(bf16[512,1024]{1,0:T(8,128)(2,1)} %get-tuple-element.8.refs_0_, bf16[512,1024]{1,0:T(8,128)(2,1)} %get-tuple-element.9.refs_1_, bf16[512,1024]{1,0:T(8,128)(2,1)} %get-tuple-element.10.refs_2_, ...), custom_call_target="tpu_custom_call" | custom-call | tf_op jit(solution)/shard_map/pallas_call | solution.py:769
